TPU v7x, 512 devices: a whole 4x4x16 slice. The times are simulated.
512 devices in a mesh: col: 32 (over z, core), row: 16 (over y, x).
Axes of the slice: x: 4, y: 4, z: 16, core: 2. Of those that a mesh axis runs over, the one named last changes fastest.
Arguments:
- panel: bfloat16 [32, 512, 1024], P('row', 'col'), may hold values from -2.5 to 2.5
- dblocks: bfloat16 [2, 512, 512], replicated, may hold values from -4 to 4, as said below
- dense_tiles: bfloat16 [16384, 16384], P('row', 'col'), may hold values from -6 to 6
- left_factor: bfloat16 [32, 64, 16384], P('col', None, 'row'), may hold values from -0.75 to 0.75
- right_factor: bfloat16 [32, 64, 16384], P('row', None, 'col'), may hold values from -6 to 6
- sketch: bfloat16 [64, 16384], P(None, 'col'), may hold values from -0.25 to 0.25
- pattern: int32 [32, 32], replicated, may hold values 0 or 1
- colmap: int32 [32], replicated, may hold values from 0 to 31, each once
Outputs:
- dense_out: bfloat16 [16384, 16384], P('row', 'col')
- sketch_out: bfloat16 [32, 64, 16384], P('col', None, 'row')
Inputs may be any that keep to these rules, and one draw needn't show every extreme that they name: `dblocks`: each of the 2 blocks is symmetric. `colmap`: every panel tile appears once.
All inputs are finite; a program needn't handle non-finite values.
Results may differ from a plain program's by a relative error of at most 0.0055.
Values may be sent and summed in bfloat16 or wider, within the bound.
No kernel may reach another device: no remote copies, remote signals or barrier semaphores. Data moves between devices by JAX's collectives and lax.ppermute only.
A program may use at most 64 MiB of HBM per device.

v0:
```python
import jax
import jax.numpy as jnp
from jax import lax
from jax.sharding import PartitionSpec as P


def spread(array, axis, root):
    mine = lax.axis_index(axis) == root
    return lax.psum(jnp.where(mine, array, jnp.zeros_like(array)), axis)


def apply_blocks(rows, dblocks):
    block_count, tile_size, _ = dblocks.shape
    leading = rows.shape[:-1]
    reshaped = rows.reshape(leading + (block_count, tile_size))
    product = jnp.einsum("...pq,pqr->...pr", reshaped, dblocks, preferred_element_type=jnp.float32)
    return product.reshape(leading + (block_count * tile_size,)).astype(jnp.bfloat16)


def update_tile(tiles, scaled, column_rows, tile_pos):
    product = lax.dot_general(
        scaled[tile_pos], column_rows, (((1,), (1,)), ((), ())), preferred_element_type=jnp.float32
    )
    return (tiles[tile_pos].astype(jnp.float32) - product).astype(jnp.bfloat16)


def empty_tile(tile_size):
    return jnp.zeros((tile_size, tile_size), jnp.bfloat16)


def on_device(panel, dblocks, dense_tiles, left_factor, right_factor, sketch, pattern, colmap):
    tile_count = panel.shape[0]
    tile_size = dblocks.shape[1]
    rank_width = sketch.shape[0]
    col_index = lax.axis_index("col")
    row_index = lax.axis_index("row")
    front_col = colmap[col_index]
    root_row = front_col // tile_count
    local_slot = front_col % tile_count
    gathered = lax.all_gather(panel, "col", axis=1, tiled=True)
    scaled = apply_blocks(gathered, dblocks)
    chosen = lax.dynamic_index_in_dim(gathered, local_slot, 0, keepdims=False)
    column_rows = spread(chosen, "row", root_row)
    pattern_col = lax.dynamic_index_in_dim(pattern, col_index, 1, keepdims=False)
    local_flags = lax.dynamic_slice_in_dim(pattern_col, row_index * tile_count, tile_count)
    projected = lax.dot_general(
        column_rows, sketch, (((0,), (1,)), ((), ())), preferred_element_type=jnp.float32
    ).astype(jnp.bfloat16)
    inner_prod = jnp.einsum(
        "ikb,lb->ikl", right_factor, sketch, preferred_element_type=jnp.float32
    ).astype(jnp.bfloat16)
    left_bases = left_factor[0].reshape(rank_width, tile_count, tile_size)
    first_term = jnp.einsum(
        "ikl,kib->lib", inner_prod, left_bases, preferred_element_type=jnp.float32
    )
    flat_scaled = scaled.reshape(tile_count * tile_size, scaled.shape[2])
    second_term = lax.dot_general(
        projected, flat_scaled, (((0,), (1,)), ((), ())), preferred_element_type=jnp.float32
    )
    sketched = (first_term.reshape(rank_width, tile_count * tile_size) - second_term).astype(
        jnp.bfloat16
    )
    sketched = sketched.reshape(rank_width, tile_count, tile_size)
    sketched = jnp.where(local_flags[None, :, None] == 1, sketched, jnp.zeros_like(sketched))
    sketch_out = sketched.reshape(1, rank_width, tile_count * tile_size)
    tiles = dense_tiles.reshape(tile_count, tile_size, tile_size)
    updated_list = []
    for tile_pos in range(tile_count):
        updated = jnp.where(
            local_flags[tile_pos] == 1,
            empty_tile(tile_size),
            update_tile(tiles, scaled, column_rows, tile_pos),
        )
        updated_list.append(updated)
    dense_out = jnp.concatenate(updated_list, axis=0)
    return (dense_out, sketch_out)


def solution(mesh):
    in_specs = (
        P("row", "col", None),
        P(),
        P("row", "col"),
        P("col", None, "row"),
        P("row", None, "col"),
        P(None, "col"),
        P(),
        P(),
    )
    out_specs = (P("row", "col"), P("col", None, "row"))
    return jax.shard_map(
        on_device, mesh=mesh, in_specs=in_specs, out_specs=out_specs, check_vma=False
    )
```

profile of v0, /device:TPU:1, one launch (start us, length us, event | category | flops | bytes accessed | tf_op | source)
XLA Modules:
  0.0 220.6 jit_solution(17422506021000322461)
XLA Ops:
  7.2 0.0 copy-start
  7.2 0.0 all-gather.2.cloned.1.call-start
  7.2 1.6 copy.26
  8.8 0.0 all-gather.2.cloned.1.call-update
  8.9 0.0 all-reduce.2.cloned.1.call-start
  8.9 1.2 dynamic_slice.13
  12.8 75.5 %all-gather.2.cloned.1.call-done = bf16[2,512,1024]{2,0,1:T(2,128)(2,1)} async-done(((bf16[2,16,1024]{2,0,1:T(2,128)(2,1)}), bf16[2,512,1024]{2,0,1:T(2,128)(2,1)}) %all-gather.2.cloned.1.call-update) | async-done | bytes 2097168 | tf_op jit(solution)/shard_map/all_gather | solution.py:40
  88.3 3.8 %constant_dynamic-slice_fusion = bf16[1,512,1024]{2,0,1:T(2,128)(2,1)S(1)} fusion(bf16[2,512,1024]{2,0,1:T(2,128)(2,1)} %all-gather.2.cloned.1.call-done, s32[]{:T(128)S(6)} %select_n.68), kind=kLoop, calls=%fused_computation.23 | loop fusion | bytes 2097156 | tf_op jit(solution)/shard_map/jit(dynamic_index_in_dim)/dynamic_slice | solution.py:42
  92.0 0.0 copy-start.8
  92.0 0.0 copy-start.1
  92.1 1.4 fusion.11
  93.5 0.0 all-reduce.2.cloned.1.call-update
  93.5 0.9 compare_reduce_fusion
  94.4 0.1 broadcast_in_dim.20
  94.5 0.0 copy-done.8
  94.5 0.1 reshape_squeeze.3
  94.6 1.3 convolution_bitcast_fusion
  95.9 0.7 copy.42
  96.6 0.5 fusion.17
  98.5 0.0 copy-done.1
  98.5 4.6 %copy.27 = bf16[2,512,1024]{1,2,0:T(8,128)(2,1)} copy(bf16[2,512,1024]{2,0,1:T(2,128)(2,1)S(1)} %copy-done.1) | data formatting | bytes 4194304 | tf_op jit(solution)/shard_map/all_gather | solution.py:40
  103.0 0.0 copy-done
  103.0 2.9 %convert_bitcast_fusion = bf16[2,512,2,512]{1,3,0,2:T(8,128)(2,1)S(1)} fusion(bf16[2,512,2,512]{1,3,2,0:T(8,128)(2,1)} %bitcast.38, bf16[2,512,512]{2,1,0:T(8,128)(2,1)S(1)} %copy-done), kind=kOutput, calls=%fused_computation.2 | convolution fusion | flops 1074790400 | bytes 5242880 | tf_op jit(solution)/shard_map/...pq,pqr->...pr/dot_general | solution.py:16
  105.9 0.0 copy-start.2
  105.9 4.2 %copy.34 = bf16[2,512,2,512]{3,2,1,0:T(2,128)(2,1)} copy(bf16[2,512,2,512]{1,3,0,2:T(8,128)(2,1)S(1)} %convert_bitcast_fusion) | data formatting | bytes 4194304 | tf_op jit(solution)/shard_map/convert_element_type | solution.py:17
  110.1 0.0 copy-done.2
  110.1 0.0 copy-start.3
  110.1 2.3 %copy.43 = bf16[128,8,2,512]{3,1,2,0:T(8,128)(2,1)S(1)} copy(bf16[128,8,2,512]{3,2,1,0:T(2,128)(2,1)} %bitcast.37) | data formatting | bytes 4194304
  112.5 0.0 copy-done.3
  112.5 1.5 fusion.16
  113.9 92.5 %all-reduce.2.cloned.1.call-done = bf16[512,1024]{1,0:T(8,128)(2,1)} async-done(((bf16[512,1024]{1,0:T(8,128)(2,1)}), bf16[512,1024]{1,0:T(8,128)(2,1)}) %all-reduce.2.cloned.1.call-update) | async-done | bytes 1048592 | tf_op jit(solution)/shard_map/psum | solution.py:9
  206.4 0.0 copy-start.4
  206.4 0.0 copy-start.5
  206.4 0.0 copy-start.9
  206.4 2.6 %fusion.7 = bf16[512,512]{1,0:T(8,128)(2,1)S(1)} fusion(bf16[512,1024]{0,1:T(8,128)(2,1)} %bitcast.40, bf16[512,1024]{1,0:T(8,128)(2,1)} %all-reduce.2.cloned.1.call-done, bf16[1024,512]{1,0:T(8,128)(2,1)} %param.10, pred[]{:T(512)} %bitcast), kind=kOutput, calls=%fused_computation.8 | convolution fusion | flops 537919488 | bytes 3145729 | tf_op jit(solution)/shard_map/dot_general | solution.py:21
  209.0 0.0 copy-done.4
  209.0 0.0 copy-done.5
  209.0 0.0 copy-done.9
  209.1 0.8 fusion.6
  209.8 0.0 copy-start.6
  209.8 0.0 copy-start.7
  209.9 1.0 pad_maximum_fusion
  210.9 0.0 copy-done.6
  210.9 0.0 copy-done.7
  210.9 2.8 %fusion.10 = bf16[1,64,1024]{2,1,0:T(8,128)(2,1)} fusion(f32[64,1024]{1,0:T(8,128)S(1)} %bitcast.41, bf16[1024,1024]{1,0:T(8,128)(2,1)S(1)} %bitcast.36, bf16[64,512]{1,0:T(8,128)(2,1)S(1)} %copy-done.7, bf16[512,1024]{1,0:T(8,128)(2,1)} %all-reduce.2.cloned.1.call-done, pred[1024]{0:T(1024)(128)(4,1)S(1)} %broadcast_in_dim.21), kind=kOutput, calls=%fused_computation.14 | convolution fusion | flops 201588736 | bytes 3605504 | tf_op jit(solution)/shard_map/dot_general | solution.py:57
  (1 shorter events, 0.0 us)
Async XLA Ops:
  7.2 95.9 %copy-start = (bf16[2,512,512]{2,1,0:T(8,128)(2,1)S(1)}, bf16[2,512,512]{2,1,0:T(8,128)(2,1)}, u32[]{:S(2)}) copy-start(bf16[2,512,512]{2,1,0:T(8,128)(2,1)} %param.9) | copy-start | bytes 3145732
  7.2 81.1 %all-gather.2.cloned.1.call-start = ((), (), s32[]{:S(2)}) async-start(), calls=%async_computation | async-start | bytes 2162688 | tf_op jit(solution)/shard_map/all_gather | solution.py:40
  8.9 197.6 %all-reduce.2.cloned.1.call-start = ((), (), s32[]{:S(2)}) async-start(), calls=%async_computation.1 | async-start | bytes 2097152 | tf_op jit(solution)/shard_map/psum | solution.py:9
  92.0 2.5 %copy-start.8 = (bf16[1,64,1024]{2,1,0:T(8,128)(2,1)S(1)}, bf16[1,64,1024]{2,1,0:T(8,128)(2,1)}, u32[]{:S(2)}) copy-start(bf16[1,64,1024]{2,1,0:T(8,128)(2,1)} %param.11) | copy-start | bytes 393220
  92.0 6.4 %copy-start.1 = (bf16[2,512,1024]{2,0,1:T(2,128)(2,1)S(1)}, bf16[2,512,1024]{2,0,1:T(2,128)(2,1)}, u32[]{:S(2)}) copy-start(bf16[2,512,1024]{2,0,1:T(2,128)(2,1)} %all-gather.2.cloned.1.call-done) | copy-start | bytes 6291460
  105.9 4.2 %copy-start.2 = (bf16[2,512,2,512]{1,3,0,2:T(8,128)(2,1)}, bf16[2,512,2,512]{1,3,0,2:T(8,128)(2,1)S(1)}, u32[]{:S(2)}) copy-start(bf16[2,512,2,512]{1,3,0,2:T(8,128)(2,1)S(1)} %convert_bitcast_fusion) | copy-start | bytes 6291460
  110.1 2.3 %copy-start.3 = (bf16[2,512,2,512]{1,3,0,2:T(8,128)(2,1)S(1)}, bf16[2,512,2,512]{1,3,0,2:T(8,128)(2,1)}, u32[]{:S(2)}) copy-start(bf16[2,512,2,512]{1,3,0,2:T(8,128)(2,1)} %copy-done.2) | copy-start | bytes 6291460
  206.4 2.6 %copy-start.4 = (bf16[512,1024]{1,0:T(8,128)(2,1)S(1)}, bf16[512,1024]{1,0:T(8,128)(2,1)}, u32[]{:S(2)}) copy-start(bf16[512,1024]{1,0:T(8,128)(2,1)} %all-reduce.2.cloned.1.call-done) | copy-start | bytes 3145732
  206.4 2.6 %copy-start.5 = (bf16[1,512,2,512]{1,3,0,2:T(8,128)(2,1)S(1)}, bf16[1,512,2,512]{1,3,0,2:T(8,128)(2,1)}, u32[]{:S(2)}) copy-start(bf16[1,512,2,512]{1,3,0,2:T(8,128)(2,1)} %get-tuple-element.5) | copy-start | bytes 3145732
  206.4 2.6 %copy-start.9 = (bf16[1024,512]{1,0:T(8,128)(2,1)S(1)}, bf16[1024,512]{1,0:T(8,128)(2,1)}, u32[]{:S(2)}) copy-start(bf16[1024,512]{1,0:T(8,128)(2,1)} %param.10) | copy-start | bytes 3145732
  209.8 1.1 copy-start.6
  209.8 1.1 copy-start.7
Sparse Core Ops, SparseCore 0:
  10.7 77.5 all-gather.1
  93.6 112.7 all-reduce.1
where the time goes:
time: 221 us
  waiting for transfers between devices  168 us (76%)
  local copies, waits for them, and re-layouts  20.7 us (9%)
  between operations  18.1 us (8%)
  matrix products  10.3 us (5%)
  other arithmetic  3.35 us (2%)
    psum x1, waiting for transfers between devices, spread(): return lax.psum(jnp.where(mine, array, jnp.zeros_like(array)), axis)  92.5 us
    all_gather x1, waiting for transfers between devices, on_device(): gathered = lax.all_gather(panel, 'col', axis=1, tiled=True)  75.5 us
    all_gather x1, local copies, waits for them, and re-layouts, on_device(): gathered = lax.all_gather(panel, 'col', axis=1, tiled=True)  4.57 us
  transfers between devices with their start and end apart: 2, of which 2 were waited for; matrix products, arithmetic and copies ran while one was open for 9% of the time, Pallas kernels for 0%

commit v1 on v0

v1 whole, which is shorter than its diff:
```python
import jax
import jax.numpy as jnp
from jax import lax
from jax.experimental import pallas as pl
from jax.experimental.pallas import tpu as pltpu
from jax.sharding import PartitionSpec as P

CORES = 2
LANES = 128
HALF = 8


def z_shift(z_count, up, down):
    return [
        (z * CORES + core, (z + (up if core == 0 else down)) % z_count * CORES + core)
        for z in range(z_count)
        for core in range(CORES)
    ]


def core_swap(z_count):
    return [(i, i ^ 1) for i in range(z_count * CORES)]


def same_core(z_count):
    return [[z * CORES + core for z in range(z_count)] for core in range(CORES)]


def same_chip(z_count):
    return [[z * CORES + core for core in range(CORES)] for z in range(z_count)]


def chunk_offsets(z_count):
    offsets = [0]
    step = z_count // 2
    while step >= 1:
        offsets = offsets + [o + step for o in offsets]
        step //= 2
    return offsets


def select_kernel(colmap_ref, tiles_ref, out_ref):
    for j in range(out_ref.shape[0]):
        out_ref[j] = tiles_ref[colmap_ref[j]]


def select_tiles(tiles, colmap):
    return pl.pallas_call(
        select_kernel,
        out_shape=jax.ShapeDtypeStruct(tiles.shape, tiles.dtype),
        in_specs=[
            pl.BlockSpec(memory_space=pltpu.SMEM),
            pl.BlockSpec(memory_space=pltpu.VMEM),
        ],
        out_specs=pl.BlockSpec(memory_space=pltpu.VMEM),
        name="select_tiles",
    )(colmap, tiles)


def final_kernel(
    offsets, info_ref, own_ref, other_ref, right_ref, first_ref, tiles_ref, dense_ref, sketch_ref, rows_ref
):
    z_count = len(offsets)
    piece = own_ref.shape[2]
    slots = own_ref.shape[1]
    tile_size = z_count * CORES * piece
    z_index = info_ref[0]
    core = info_ref[1]
    for from_other, chunk_ref in ((0, own_ref), (1, other_ref)):
        owner = core ^ from_other if from_other else core
        sign = 2 * owner - 1
        for j, offset in enumerate(offsets):
            z_from = (z_index + sign * offset + z_count) & (z_count - 1)
            start = (z_from * CORES + owner) * piece
            for slot in range(slots):
                row = pl.multiple_of(slot * tile_size + start, piece)
                rows_ref[pl.ds(row, piece), :] = chunk_ref[j, slot]
    step = 256
    width = dense_ref.shape[1]

    def body(i, carry):
        row = pl.multiple_of(i * step, step)
        low = info_ref[2 + i // (tile_size // step)] == 1
        product = lax.dot_general(
            rows_ref[pl.ds(row, step), :],
            right_ref[...],
            (((1,), (1,)), ((), ())),
            preferred_element_type=jnp.float32,
        )
        updated = tiles_ref[pl.ds(row, step), :].astype(jnp.float32) - product[:, :width]
        dense_ref[pl.ds(row, step), :] = jnp.where(low, 0.0, updated).astype(dense_ref.dtype)
        sketched = first_ref[:, pl.ds(row, step)] - product[:, width:].T
        sketch_ref[:, pl.ds(row, step)] = jnp.where(low, sketched, 0.0).astype(sketch_ref.dtype)
        return carry

    lax.fori_loop(0, slots * tile_size // step, body, 0)


def final_update(info, own, other, right, first_term, dense_tiles, rank_width):
    z_count, slots, piece, depth = own.shape
    rows = z_count * CORES * slots * piece
    vmem = pl.BlockSpec(memory_space=pltpu.VMEM)

    def kernel(*refs):
        final_kernel(chunk_offsets(z_count), *refs)

    return pl.pallas_call(
        kernel,
        out_shape=(
            jax.ShapeDtypeStruct(dense_tiles.shape, dense_tiles.dtype),
            jax.ShapeDtypeStruct((rank_width, rows), dense_tiles.dtype),
        ),
        in_specs=[pl.BlockSpec(memory_space=pltpu.SMEM)] + [vmem] * 5,
        out_specs=(vmem, vmem),
        scratch_shapes=[pltpu.VMEM((rows, depth), own.dtype)],
        compiler_params=pltpu.CompilerParams(vmem_limit_bytes=40 * 1024 * 1024),
        cost_estimate=pl.CostEstimate(
            flops=2 * rows * depth * right.shape[0], bytes_accessed=8 * 1024 * 1024, transcendentals=0
        ),
        name="final_update",
    )(info, own, other, right, first_term, dense_tiles)


def on_device(panel, dblocks, dense_tiles, left_factor, right_factor, sketch, pattern, colmap):
    slots, piece, depth = panel.shape
    blocks, tile_size, _ = dblocks.shape
    rank_width = sketch.shape[0]
    col_count = tile_size // piece
    z_count = col_count // CORES
    row_count = pattern.shape[0] // slots
    col_index = lax.axis_index("col")
    row_index = lax.axis_index("row")
    z_index = col_index // CORES
    core = col_index % CORES

    scaled = jnp.einsum(
        "sapq,pqr->sapr",
        panel.reshape(slots, piece, blocks, tile_size),
        dblocks,
        preferred_element_type=jnp.float32,
    )
    own = scaled.reshape(1, slots, piece, depth).astype(jnp.bfloat16)
    step = z_count // 2
    while step >= 1:
        own = jnp.concatenate([own, lax.ppermute(own, "col", z_shift(z_count, step, -step))], axis=0)
        step //= 2
    other = lax.ppermute(own, "col", core_swap(z_count))

    lane_blocks = depth // LANES
    halves = piece // HALF
    parts = panel.reshape(slots, halves, HALF, lane_blocks, LANES).transpose(1, 3, 0, 2, 4)
    parts = parts.reshape(row_count, slots, HALF, LANES)
    parts = lax.all_to_all(parts, "row", 0, 0)
    parts = select_tiles(parts.reshape(row_count * slots, HALF, LANES), colmap)
    parts = parts.reshape(z_count, CORES, HALF, LANES)
    parts = lax.all_to_all(parts, "col", 0, 0, axis_index_groups=same_core(z_count))
    parts = lax.all_gather(parts, "col", axis=1, axis_index_groups=same_chip(z_count))
    parts = lax.dynamic_index_in_dim(parts, core, 2, keepdims=False)
    parts = parts.reshape(1, col_count, HALF, LANES)
    parts = jnp.broadcast_to(parts, (row_count, col_count, HALF, LANES))
    parts = lax.all_to_all(parts, "row", 0, 0)
    parts = parts.reshape(halves, lane_blocks, col_count, HALF, LANES).transpose(2, 0, 3, 1, 4)
    column_rows = parts.reshape(tile_size, depth)

    projected = lax.dot_general(
        sketch, column_rows, (((1,), (0,)), ((), ())), preferred_element_type=jnp.float32
    ).astype(jnp.bfloat16)
    right = jnp.concatenate([column_rows, projected], axis=0)

    inner_prod = jnp.einsum(
        "ikb,lb->ikl", right_factor, sketch, preferred_element_type=jnp.float32
    ).astype(jnp.bfloat16)
    left_bases = left_factor[0].reshape(rank_width, slots, tile_size)
    first_term = jnp.einsum(
        "ikl,kib->lib", inner_prod, left_bases, preferred_element_type=jnp.float32
    ).reshape(rank_width, slots * tile_size)

    pattern_col = lax.dynamic_index_in_dim(pattern, col_index, 1, keepdims=False)
    local_flags = lax.dynamic_slice_in_dim(pattern_col, row_index * slots, slots)
    info = jnp.concatenate([jnp.stack([z_index, core]), local_flags]).astype(jnp.int32)
    dense_out, sketch_out = final_update(
        info, own, other, right, first_term, dense_tiles, rank_width
    )
    return dense_out, sketch_out.reshape(1, rank_width, slots * tile_size)


def solution(mesh):
    in_specs = (
        P("row", "col", None),
        P(),
        P("row", "col"),
        P("col", None, "row"),
        P("row", None, "col"),
        P(None, "col"),
        P(),
        P(),
    )
    out_specs = (P("row", "col"), P("col", None, "row"))
    return jax.shard_map(
        on_device, mesh=mesh, in_specs=in_specs, out_specs=out_specs, check_vma=False
    )
```

time: 221 us -> 115 us (0.52)
  waiting for transfers between devices: 168 us -> 22.5 us
  starting transfers between devices: 0.08 us -> 52.3 us
  blocking collectives: 0 us -> 22.2 us
  between operations: 18.1 us -> 0.94 us
  local copies, waits for them, and re-layouts: 20.7 us -> 7.22 us
  matrix products: 10.3 us -> 2.6 us
  Pallas kernels: 0 us -> 5.82 us
  other arithmetic: 3.35 us -> 1.09 us
    psum x1 -> x0, waiting for transfers between devices: 92.5 us -> none  [spread(): return lax.psum(jnp.where(mine, array, jnp.zeros_like(array)), axis)]
    all_gather x1 -> x0, waiting for transfers between devices: 75.5 us -> none  [on_device(): gathered = lax.all_gather(panel, 'col', axis=1, tiled=True)]
    ppermute x0 -> x5, starting transfers between devices: none -> 39.3 us  [the longest x4 37 us: on_device(): lax.ppermute(own, 'col', z_shift(z_count, step, -step))]
    all_to_all x0 -> x2, waiting for transfers between devices: none -> 16.9 us  [the longest x1 10.7 us: on_device(): parts = lax.all_to_all(parts, 'row', 0, 0)]
    all_to_all x0 -> x1, blocking collectives: none -> 13.2 us  [on_device(): parts = lax.all_to_all(parts, 'row', 0, 0)]
    all_to_all x0 -> x2, starting transfers between devices: none -> 13 us  [the longest x1 8.67 us: on_device(): lax.all_to_all(parts, 'col', 0, 0, axis_index_groups=same_core(z_count))]
    all_gather x0 -> x1, blocking collectives: none -> 9.05 us  [on_device(): lax.all_gather(parts, 'col', axis=1, axis_index_groups=same_chip(z_count))]
    dot_general x4 -> x1, matrix products: 9.03 us -> 0.3 us  [on_device(): lax.dot_general(sketch, column_rows, (((1,), (0,)), ((), ())), preferred_...]
  transfers between devices with their start and end apart: 2 -> 7, of which waited for: 2 -> 4; matrix products, arithmetic and copies ran while one was open for 9% -> 7% of each run, Pallas kernels for 0% -> 1%
where the time goes in v1:
time: 115 us
  starting transfers between devices  52.3 us (45%)
  waiting for transfers between devices  22.5 us (20%)
  blocking collectives  22.2 us (19%)
  local copies, waits for them, and re-layouts  7.22 us (6%)
  Pallas kernels  5.82 us (5%)
  matrix products  2.6 us (2%)
    ppermute x4, starting transfers between devices, on_device(): lax.ppermute(own, 'col', z_shift(z_count, step, -step))  37 us
    all_to_all x1, blocking collectives, on_device(): parts = lax.all_to_all(parts, 'row', 0, 0)  13.2 us
    all_to_all x1, waiting for transfers between devices, on_device(): parts = lax.all_to_all(parts, 'row', 0, 0)  10.7 us
    all_gather x1, blocking collectives, on_device(): lax.all_gather(parts, 'col', axis=1, axis_index_groups=same_chip(z_count))  9.05 us
    all_to_all x1, starting transfers between devices, on_device(): lax.all_to_all(parts, 'col', 0, 0, axis_index_groups=same_core(z_count))  8.67 us
    all_to_all x1, waiting for transfers between devices, on_device(): lax.all_to_all(parts, 'col', 0, 0, axis_index_groups=same_core(z_count))  6.2 us
    ppermute x4, waiting for transfers between devices, on_device(): lax.ppermute(own, 'col', z_shift(z_count, step, -step))  5.63 us
    all_to_all x1, starting transfers between devices, on_device(): parts = lax.all_to_all(parts, 'row', 0, 0)  4.35 us
  transfers between devices with their start and end apart: 7, of which 4 were waited for; matrix products, arithmetic and copies ran while one was open for 7% of the time, Pallas kernels for 1%

profile of v1, /device:TPU:1, one launch (start us, length us, event | category | flops | bytes accessed | tf_op | source)
XLA Modules:
  0.0 114.7 jit_solution(2374224881807077387)
XLA Ops:
  0.6 0.0 copy-start
  0.6 0.9 copy.26
  1.6 0.3 copy-done
  1.9 0.0 copy-start.3
  1.9 0.3 fusion.4
  2.2 0.1 copy.16
  2.3 16.3 %collective-permute-start = (bf16[1,2,16,1024]{3,2,1,0:T(8,128)(2,1)S(1)}, bf16[1,2,16,1024]{3,2,1,0:T(8,128)(2,1)S(1)}, u32[]{:S(2)}, u32[]{:S(2)}) collective-permute-start(bf16[1,2,16,1024]{3,2,1,0:T(8,128)(2,1)S(1)} %convert_element_type.28), channel_id=1, source_target_pairs={{0,256},{16,272},{32,288},{48,304},{64,320},{80,336},{96,352},{112... | collective-permute-start | bytes 196616 | tf_op jit(solution)/shard_map/ppermute | solution.py:145
  18.6 1.8 %collective-permute-done = bf16[1,2,16,1024]{3,2,1,0:T(8,128)(2,1)S(1)} collective-permute-done((bf16[1,2,16,1024]{3,2,1,0:T(8,128)(2,1)S(1)}, bf16[1,2,16,1024]{3,2,1,0:T(8,128)(2,1)S(1)}, u32[]{:S(2)}, u32[]{:S(2)}) %collective-permute-start) | collective-permute-done | bytes 65568 | tf_op jit(solution)/shard_map/ppermute | solution.py:145
  20.5 8.9 %collective-permute-start.1 = (bf16[2,2,16,1024]{3,2,1,0:T(8,128)(2,1)S(1)}, bf16[2,2,16,1024]{3,2,1,0:T(8,128)(2,1)S(1)}, u32[]{:S(2)}, u32[]{:S(2)}) collective-permute-start(bf16[2,2,16,1024]{3,2,1,0:T(8,128)(2,1)S(1)} %pad_maximum_fusion.3), channel_id=1, source_target_pairs={{0,128},{16,400},{32,160},{48,432},{64,192},{80,464},{96,224},{112... | collective-permute-start | bytes 393224 | tf_op jit(solution)/shard_map/ppermute | solution.py:145
  29.4 3.8 %collective-permute-done.1 = bf16[2,2,16,1024]{3,2,1,0:T(8,128)(2,1)S(1)} collective-permute-done((bf16[2,2,16,1024]{3,2,1,0:T(8,128)(2,1)S(1)}, bf16[2,2,16,1024]{3,2,1,0:T(8,128)(2,1)S(1)}, u32[]{:S(2)}, u32[]{:S(2)}) %collective-permute-start.1) | collective-permute-done | bytes 131104 | tf_op jit(solution)/shard_map/ppermute | solution.py:145
  33.2 7.4 %collective-permute-start.2 = (bf16[4,2,16,1024]{3,2,1,0:T(8,128)(2,1)S(1)}, bf16[4,2,16,1024]{3,2,1,0:T(8,128)(2,1)S(1)}, u32[]{:S(2)}, u32[]{:S(2)}) collective-permute-start(bf16[4,2,16,1024]{3,2,1,0:T(8,128)(2,1)S(1)} %pad_maximum_fusion.2), channel_id=1, source_target_pairs={{0,64},{16,464},{32,96},{48,496},{64,128},{80,16},{96,160},{112,48... | collective-permute-start | bytes 786440 | tf_op jit(solution)/shard_map/ppermute | solution.py:145
  40.6 0.0 copy-done.3
  40.6 13.2 %all_to_all.15 = bf16[16,2,8,128]{3,2,1,0:T(8,128)(2,1)} all-to-all(bf16[16,2,8,128]{3,2,1,0:T(8,128)(2,1)S(1)} %bitcast.51), channel_id=1, replica_groups=mesh['col'=32,'row'=16] {'row'}, dimensions={0} | all-to-all | bytes 131072 | tf_op jit(solution)/shard_map/all_to_all | solution.py:153
  53.8 1.5 %select_tiles.1 = bf16[32,8,128]{2,1,0:T(8,128)(2,1)} custom-call(s32[32]{0:T(128)} %colmap_ref.1, bf16[32,8,128]{2,1,0:T(8,128)(2,1)} %bitcast.50), custom_call_target="tpu_custom_call" | custom-call | tf_op jit(solution)/shard_map/select_tiles/pallas_call | solution.py:48
  55.3 8.7 %all-to-all-start.1 = ((bf16[16,2,8,128]{3,2,1,0:T(8,128)(2,1)}), bf16[16,2,8,128]{3,2,1,0:T(8,128)(2,1)S(1)}, u32[]{:S(2)}, u32[]{:S(2)}) async-start(bf16[16,2,8,128]{3,2,1,0:T(8,128)(2,1)} %bitcast.49), calls=%async_computation.1 | async-start | bytes 131072 | tf_op jit(solution)/shard_map/all_to_all | solution.py:156
  64.0 0.0 collective-permute-done.2
  64.0 0.9 pad_maximum_fusion.1
  64.8 4.5 %collective-permute-start.3 = (bf16[8,2,16,1024]{3,2,1,0:T(8,128)(2,1)}, bf16[8,2,16,1024]{3,2,1,0:T(8,128)(2,1)S(1)}, u32[]{:S(2)}, u32[]{:S(2)}) collective-permute-start(bf16[8,2,16,1024]{3,2,1,0:T(8,128)(2,1)} %pad_maximum_fusion.1), channel_id=1, source_target_pairs={{0,32},{16,496},{32,64},{48,16},{64,96},{80,48},{96,128},{112,80},... | collective-permute-start | bytes 1572872 | tf_op jit(solution)/shard_map/ppermute | solution.py:145
  69.4 6.2 %all-to-all-done.1 = bf16[16,2,8,128]{3,2,1,0:T(8,128)(2,1)S(1)} async-done(((bf16[16,2,8,128]{3,2,1,0:T(8,128)(2,1)}), bf16[16,2,8,128]{3,2,1,0:T(8,128)(2,1)S(1)}, u32[]{:S(2)}, u32[]{:S(2)}) %all-to-all-start.1) | async-done | bytes 65568 | tf_op jit(solution)/shard_map/all_to_all | solution.py:156
  75.6 9.1 %all-gather = bf16[16,4,8,128]{3,2,1,0:T(8,128)(2,1)S(1)} all-gather(bf16[16,2,8,128]{3,2,1,0:T(8,128)(2,1)S(1)} %all-to-all-done.1), channel_id=2, replica_groups={{0,16},{32,48},{64,80},{96,112},{128,144},{160,176},{192,208},{224,240}..., dimensions={1}, use_global_device_ids=true | all-gather | bytes 196608 | tf_op jit(solution)/shard_map/all_gather | solution.py:157
  84.7 1.2 %broadcast_in_dim.8 = bf16[16,32,8,128]{3,2,1,0:T(8,128)(2,1)} broadcast(bf16[32,8,128]{2,1,0:T(8,128)(2,1)S(1)} %bitcast.45), dimensions={1,2,3} | broadcast | bytes 1114112 | tf_op jit(solution)/shard_map/broadcast_in_dim | solution.py:160
  85.8 4.4 %all-to-all-start.2 = ((bf16[16,32,8,128]{3,2,1,0:T(8,128)(2,1)}), bf16[16,32,8,128]{3,2,1,0:T(8,128)(2,1)}, u32[]{:S(2)}, u32[]{:S(2)}) async-start(bf16[16,32,8,128]{3,2,1,0:T(8,128)(2,1)} %broadcast_in_dim.8), calls=%async_computation.2 | async-start | bytes 2097152 | tf_op jit(solution)/shard_map/all_to_all | solution.py:161
  90.2 0.0 copy-start.4
  90.2 0.0 copy-start.2
  90.3 0.0 collective-permute-done.3
  90.3 2.3 %collective-permute-start.4 = (bf16[16,2,16,1024]{3,2,1,0:T(8,128)(2,1)S(1)}, bf16[16,2,16,1024]{3,2,1,0:T(8,128)(2,1)S(1)}, u32[]{:S(2)}, u32[]{:S(2)}) collective-permute-start(bf16[16,2,16,1024]{3,2,1,0:T(8,128)(2,1)S(1)} %constant_dynamic-update-slice_fusion.refs_1_), channel_id=1, source_target_pairs={{0,16},{16,0},{32,48},{48,32},{64,80},{80,64},{96,112},{112,96},{1... | collective-permute-start | bytes 3145736 | tf_op jit(solution)/shard_map/ppermute | solution.py:147
  92.6 0.0 copy-done.4
  92.6 0.1 reshape_squeeze.3
  92.7 0.0 copy-done.2
  92.7 2.0 %convolution_bitcast_fusion = f32[2,8,8,512]{3,2,1,0:T(8,128)} fusion(bf16[2,64,512]{2,1,0:T(8,128)(2,1)} %param.12, bf16[64,2,512]{2,1,0:T(2,128)(2,1)S(1)} %reshape_squeeze.3, bf16[64,512]{1,0:T(8,128)(2,1)S(1)} %copy-done.2), kind=kOutput, calls=%fused_computation.1 | convolution fusion | flops 16785408 | bytes 589824 | tf_op jit(solution)/shard_map/ikl,kib->lib/dot_general | solution.py:174
  94.7 1.0 copy.22
  95.7 0.9 dynamic-slice_reduce_fusion
  96.6 0.1 pad_add_fusion.refs_0_
  96.7 10.7 %all-to-all-done.2 = bf16[16,32,8,128]{3,2,1,0:T(8,128)(2,1)} async-done(((bf16[16,32,8,128]{3,2,1,0:T(8,128)(2,1)}), bf16[16,32,8,128]{3,2,1,0:T(8,128)(2,1)}, u32[]{:S(2)}, u32[]{:S(2)}) %all-to-all-start.2) | async-done | bytes 1048608 | tf_op jit(solution)/shard_map/all_to_all | solution.py:161
  107.4 1.5 %copy.18 = bf16[2,8,32,8,128]{4,3,1,0,2:T(8,128)(2,1)S(1)} copy(bf16[2,8,32,8,128]{4,3,2,1,0:T(8,128)(2,1)} %bitcast.13) | data formatting | bytes 2097152 | tf_op jit(solution)/shard_map/reshape | solution.py:162
  108.9 0.3 fusion
  109.2 0.0 copy-start.1
  109.2 0.1 pad_maximum_fusion.refs_3_
  109.3 0.0 collective-permute-done.4.refs_2_
  109.3 1.1 copy-done.1
  110.4 4.3 %final_update.1 = (bf16[1024,512]{1,0:T(8,128)(2,1)}, bf16[64,1024]{1,0:T(8,128)(2,1)}) custom-call(s32[4]{0:T(128)S(1)} %pad_add_fusion.refs_0_, bf16[16,2,16,1024]{3,2,1,0:T(8,128)(2,1)S(1)} %constant_dynamic-update-slice_fusion.refs_1_, bf16[16,2,16,1024]{3,2,1,0:T(8,128)(2,1)S(1)} %collective-permute-done.4.refs_2_, ...), custom_call_target="tpu_custom_call" | custom-call | flops 1207959552 | bytes 8388608 | tf_op jit(solution)/shard_map/final_update/pallas_call | solution.py:107
  (11 shorter events, 0.2 us)
Async XLA Ops:
  0.6 1.3 %copy-start = (bf16[2,512,512]{2,1,0:T(8,128)(2,1)S(1)}, bf16[2,512,512]{2,1,0:T(8,128)(2,1)}, u32[]{:S(2)}) copy-start(bf16[2,512,512]{2,1,0:T(8,128)(2,1)} %param.9) | copy-start | bytes 3145732
  1.9 38.7 %copy-start.3 = (bf16[2,16,1024]{2,1,0:T(8,128)(2,1)S(1)}, bf16[2,16,1024]{2,1,0:T(8,128)(2,1)}, u32[]{:S(2)}) copy-start(bf16[2,16,1024]{2,1,0:T(8,128)(2,1)} %param.8) | copy-start | bytes 196612
  2.3 18.1 %collective-permute-start = (bf16[1,2,16,1024]{3,2,1,0:T(8,128)(2,1)S(1)}, bf16[1,2,16,1024]{3,2,1,0:T(8,128)(2,1)S(1)}, u32[]{:S(2)}, u32[]{:S(2)}) collective-permute-start(bf16[1,2,16,1024]{3,2,1,0:T(8,128)(2,1)S(1)} %convert_element_type.28), channel_id=1, source_target_pairs={{0,256},{16,272},{32,288},{48,304},{64,320},{80,336},{96,352},{112... | collective-permute-start | bytes 196616 | tf_op jit(solution)/shard_map/ppermute | solution.py:145
  20.5 12.7 %collective-permute-start.1 = (bf16[2,2,16,1024]{3,2,1,0:T(8,128)(2,1)S(1)}, bf16[2,2,16,1024]{3,2,1,0:T(8,128)(2,1)S(1)}, u32[]{:S(2)}, u32[]{:S(2)}) collective-permute-start(bf16[2,2,16,1024]{3,2,1,0:T(8,128)(2,1)S(1)} %pad_maximum_fusion.3), channel_id=1, source_target_pairs={{0,128},{16,400},{32,160},{48,432},{64,192},{80,464},{96,224},{112... | collective-permute-start | bytes 393224 | tf_op jit(solution)/shard_map/ppermute | solution.py:145
  33.2 30.8 %collective-permute-start.2 = (bf16[4,2,16,1024]{3,2,1,0:T(8,128)(2,1)S(1)}, bf16[4,2,16,1024]{3,2,1,0:T(8,128)(2,1)S(1)}, u32[]{:S(2)}, u32[]{:S(2)}) collective-permute-start(bf16[4,2,16,1024]{3,2,1,0:T(8,128)(2,1)S(1)} %pad_maximum_fusion.2), channel_id=1, source_target_pairs={{0,64},{16,464},{32,96},{48,496},{64,128},{80,16},{96,160},{112,48... | collective-permute-start | bytes 786440 | tf_op jit(solution)/shard_map/ppermute | solution.py:145
  55.3 20.3 %all-to-all-start.1 = ((bf16[16,2,8,128]{3,2,1,0:T(8,128)(2,1)}), bf16[16,2,8,128]{3,2,1,0:T(8,128)(2,1)S(1)}, u32[]{:S(2)}, u32[]{:S(2)}) async-start(bf16[16,2,8,128]{3,2,1,0:T(8,128)(2,1)} %bitcast.49), calls=%async_computation.1 | async-start | bytes 131072 | tf_op jit(solution)/shard_map/all_to_all | solution.py:156
  64.8 25.4 %collective-permute-start.3 = (bf16[8,2,16,1024]{3,2,1,0:T(8,128)(2,1)}, bf16[8,2,16,1024]{3,2,1,0:T(8,128)(2,1)S(1)}, u32[]{:S(2)}, u32[]{:S(2)}) collective-permute-start(bf16[8,2,16,1024]{3,2,1,0:T(8,128)(2,1)} %pad_maximum_fusion.1), channel_id=1, source_target_pairs={{0,32},{16,496},{32,64},{48,16},{64,96},{80,48},{96,128},{112,80},... | collective-permute-start | bytes 1572872 | tf_op jit(solution)/shard_map/ppermute | solution.py:145
  85.8 21.5 %all-to-all-start.2 = ((bf16[16,32,8,128]{3,2,1,0:T(8,128)(2,1)}), bf16[16,32,8,128]{3,2,1,0:T(8,128)(2,1)}, u32[]{:S(2)}, u32[]{:S(2)}) async-start(bf16[16,32,8,128]{3,2,1,0:T(8,128)(2,1)} %broadcast_in_dim.8), calls=%async_computation.2 | async-start | bytes 2097152 | tf_op jit(solution)/shard_map/all_to_all | solution.py:161
  90.2 2.4 %copy-start.4 = (bf16[1,64,1024]{2,1,0:T(8,128)(2,1)S(1)}, bf16[1,64,1024]{2,1,0:T(8,128)(2,1)}, u32[]{:S(2)}) copy-start(bf16[1,64,1024]{2,1,0:T(8,128)(2,1)} %param.11) | copy-start | bytes 393220
  90.2 2.5 %copy-start.2 = (bf16[64,512]{1,0:T(8,128)(2,1)S(1)}, bf16[64,512]{1,0:T(8,128)(2,1)}, u32[]{:S(2)}) copy-start(bf16[64,512]{1,0:T(8,128)(2,1)} %param.13) | copy-start | bytes 196612
  90.3 19.0 %collective-permute-start.4 = (bf16[16,2,16,1024]{3,2,1,0:T(8,128)(2,1)S(1)}, bf16[16,2,16,1024]{3,2,1,0:T(8,128)(2,1)S(1)}, u32[]{:S(2)}, u32[]{:S(2)}) collective-permute-start(bf16[16,2,16,1024]{3,2,1,0:T(8,128)(2,1)S(1)} %constant_dynamic-update-slice_fusion.refs_1_), channel_id=1, source_target_pairs={{0,16},{16,0},{32,48},{48,32},{64,80},{80,64},{96,112},{112,96},{1... | collective-permute-start | bytes 3145736 | tf_op jit(solution)/shard_map/ppermute | solution.py:147
  109.2 1.2 %copy-start.1 = (bf16[1024,512]{1,0:T(8,128)(2,1)S(1)}, bf16[1024,512]{1,0:T(8,128)(2,1)}, u32[]{:S(2)}) copy-start(bf16[1024,512]{1,0:T(8,128)(2,1)} %refs_5_.1) | copy-start | bytes 3145732

commit v2 on v1

v2 whole, which is shorter than its diff:
```python
import jax
import jax.numpy as jnp
from jax import lax
from jax.experimental import pallas as pl
from jax.experimental.pallas import tpu as pltpu
from jax.sharding import PartitionSpec as P

CORES = 2
LANES = 128
HALF = 8
ROW_STEP = 512
VMEM = pl.BlockSpec(memory_space=pltpu.VMEM)
SMEM = pl.BlockSpec(memory_space=pltpu.SMEM)
ANY = pl.BlockSpec(memory_space=pl.ANY)


def z_shift(z_count, up, down):
    return [
        (z * CORES + core, (z + (up if core == 0 else down)) % z_count * CORES + core)
        for z in range(z_count)
        for core in range(CORES)
    ]


def core_swap(z_count):
    return [(i, i ^ 1) for i in range(z_count * CORES)]


def same_core(z_count):
    return [[z * CORES + core for z in range(z_count)] for core in range(CORES)]


def same_chip(z_count):
    return [[z * CORES + core for core in range(CORES)] for z in range(z_count)]


def shift(array, z_count, up, down):
    return lax.ppermute(array, "col", z_shift(z_count, up, down))


def chunk_offsets(z_count):
    half, quarter = z_count // 2, z_count // 4
    return [
        (near[0] + far[0], near[1] + far[1])
        for near in ((0, 0), (-1, 0), (1, 0), (0, 2))
        for far in ((0, 0), (half, 0), (0, quarter), (half, quarter))
    ]


def stack_kernel(*refs):
    *chunk_refs, _, out_ref = refs
    count = chunk_refs[0].shape[0]
    for j, chunk_ref in enumerate(chunk_refs):
        out_ref[j * count : (j + 1) * count] = chunk_ref[...]


def stack_after(chunks, earlier):
    shape = (len(chunks) * chunks[0].shape[0],) + chunks[0].shape[1:]
    return pl.pallas_call(
        stack_kernel,
        out_shape=jax.ShapeDtypeStruct(shape, chunks[0].dtype),
        in_specs=[VMEM] * (len(chunks) + 1),
        out_specs=VMEM,
        compiler_params=pltpu.CompilerParams(vmem_limit_bytes=2 * 1024 * 1024),
        name="stack_after",
    )(*chunks, earlier)


def same_kernel(*refs):
    pass


def hold(array, *earlier):
    return pl.pallas_call(
        same_kernel,
        out_shape=jax.ShapeDtypeStruct(array.shape, array.dtype),
        in_specs=[VMEM] * (1 + len(earlier)),
        out_specs=VMEM,
        input_output_aliases={0: 0},
        compiler_params=pltpu.CompilerParams(vmem_limit_bytes=1024 * 1024),
        name="hold",
    )(array, *earlier)


def select_kernel(colmap_ref, tiles_ref, _, out_ref):
    for j in range(out_ref.shape[0]):
        out_ref[j] = tiles_ref[colmap_ref[j]]


def select_tiles(tiles, colmap, earlier):
    return pl.pallas_call(
        select_kernel,
        out_shape=jax.ShapeDtypeStruct(tiles.shape, tiles.dtype),
        in_specs=[SMEM, VMEM, VMEM],
        out_specs=VMEM,
        compiler_params=pltpu.CompilerParams(vmem_limit_bytes=1024 * 1024),
        name="select_tiles",
    )(colmap, tiles, earlier)


def order_kernel(offsets, info_ref, own_ref, other_ref, rows_ref):
    z_count = len(offsets)
    _, slots, piece, _ = own_ref.shape
    tile_size = z_count * CORES * piece
    z_index = info_ref[0]
    core = info_ref[1]
    for owner, chunk_ref in ((core, own_ref), (1 - core, other_ref)):
        sign = 2 * owner - 1
        for j, (fixed, mirrored) in enumerate(offsets):
            z_from = (z_index + fixed + sign * mirrored + z_count) & (z_count - 1)
            start = (z_from * CORES + owner) * piece
            for slot in range(slots):
                row = pl.multiple_of(slot * tile_size + start, piece)
                rows_ref[pl.ds(row, piece), :] = chunk_ref[j, slot]


def order_rows(info, own, other):
    z_count, slots, piece, depth = own.shape

    def kernel(*refs):
        order_kernel(chunk_offsets(z_count), *refs)

    return pl.pallas_call(
        kernel,
        out_shape=jax.ShapeDtypeStruct((CORES * z_count * slots * piece, depth), own.dtype),
        in_specs=[SMEM, VMEM, VMEM],
        out_specs=VMEM,
        compiler_params=pltpu.CompilerParams(vmem_limit_bytes=6 * 1024 * 1024),
        name="order_rows",
    )(info, own, other)


def final_kernel(
    info_ref, rows_ref, right_ref, first_ref, tiles_ref, dense_ref, sketched_ref
):
    i = pl.program_id(0)
    tile_size = dense_ref.shape[1]
    low = info_ref[2 + i * rows_ref.shape[0] // tile_size] == 1
    product = lax.dot_general(
        rows_ref[...],
        right_ref[...],
        (((1,), (1,)), ((), ())),
        preferred_element_type=jnp.float32,
    )
    updated = tiles_ref[...].astype(jnp.float32) - product[:, :tile_size]
    dense_ref[...] = jnp.where(low, 0.0, updated).astype(dense_ref.dtype)
    sketched = first_ref[...] - product[:, tile_size:].T
    sketched_ref[...] = jnp.where(low, sketched, 0.0).astype(sketched_ref.dtype)


def final_update(info, rows, right, first_term, dense_tiles):
    count, depth = rows.shape
    rank_width, tile_size = first_term.shape[0], dense_tiles.shape[1]
    return pl.pallas_call(
        final_kernel,
        grid=(count // ROW_STEP,),
        out_shape=(
            jax.ShapeDtypeStruct(dense_tiles.shape, dense_tiles.dtype),
            jax.ShapeDtypeStruct((rank_width, count), dense_tiles.dtype),
        ),
        in_specs=[
            SMEM,
            pl.BlockSpec((ROW_STEP, depth), lambda i: (i, 0)),
            VMEM,
            pl.BlockSpec((rank_width, ROW_STEP), lambda i: (0, i)),
            pl.BlockSpec((ROW_STEP, tile_size), lambda i: (i, 0)),
        ],
        out_specs=(
            pl.BlockSpec((ROW_STEP, tile_size), lambda i: (i, 0)),
            pl.BlockSpec((rank_width, ROW_STEP), lambda i: (0, i)),
        ),
        compiler_params=pltpu.CompilerParams(vmem_limit_bytes=12 * 1024 * 1024),
        cost_estimate=pl.CostEstimate(
            flops=2 * count * depth * (tile_size + rank_width),
            bytes_accessed=6 * 1024 * 1024,
            transcendentals=0,
        ),
        name="final_update",
    )(info, rows, right, first_term, dense_tiles)


def on_device(panel, dblocks, dense_tiles, left_factor, right_factor, sketch, pattern, colmap):
    slots, piece, depth = panel.shape
    blocks, tile_size, _ = dblocks.shape
    rank_width = sketch.shape[0]
    col_count = tile_size // piece
    z_count = col_count // CORES
    row_count = pattern.shape[0] // slots
    col_index = lax.axis_index("col")
    row_index = lax.axis_index("row")
    z_index = col_index // CORES
    core = col_index % CORES

    lane_blocks = depth // LANES
    halves = piece // HALF
    parts = panel.reshape(slots, halves, HALF, lane_blocks, LANES).transpose(1, 3, 0, 2, 4)
    parts = parts.reshape(row_count, slots, HALF, LANES)
    parts = lax.all_to_all(parts, "row", 0, 0)
    parts = parts.reshape(row_count * slots, HALF, LANES)

    scaled = jnp.einsum(
        "sapq,pqr->sapr",
        panel.reshape(slots, piece, blocks, tile_size),
        dblocks,
        preferred_element_type=jnp.float32,
    )
    own = scaled.reshape(1, slots, piece, depth).astype(jnp.bfloat16)
    half = shift(own, z_count, z_count // 2, z_count // 2)
    parts = select_tiles(parts, colmap, half)
    own = jnp.concatenate([own, half], axis=0)
    quarter = shift(own, z_count, z_count // 4, -(z_count // 4))
    parts = parts.reshape(z_count, CORES, HALF, LANES)
    parts = lax.all_to_all(parts, "col", 0, 0, axis_index_groups=same_core(z_count))
    own = stack_after([own, quarter], parts)
    parts = lax.all_gather(parts, "col", axis=1, axis_index_groups=same_chip(z_count))
    parts = hold(parts, own)
    parts = lax.dynamic_index_in_dim(parts, core, 2, keepdims=False)
    parts = parts.reshape(1, col_count, HALF, LANES)
    parts = jnp.broadcast_to(parts, (row_count, col_count, HALF, LANES))

    near = [shift(own, z_count, up, down) for up, down in ((1, 1), (-1, -1), (2, -2))]
    own = jnp.concatenate([own] + near, axis=0)

    parts = lax.all_to_all(parts, "row", 0, 0)
    inner_prod = jnp.einsum(
        "ikb,lb->ikl", right_factor, sketch, preferred_element_type=jnp.float32
    ).astype(jnp.bfloat16)
    left_bases = left_factor[0].reshape(rank_width, slots, tile_size)
    first_term = jnp.einsum(
        "ikl,kib->lib", inner_prod, left_bases, preferred_element_type=jnp.float32
    ).reshape(rank_width, slots * tile_size)

    own = hold(own, parts, first_term)
    other = lax.ppermute(own, "col", core_swap(z_count))
    parts = parts.reshape(halves, lane_blocks, col_count, HALF, LANES).transpose(2, 0, 3, 1, 4)
    column_rows = parts.reshape(tile_size, depth)
    projected = lax.dot_general(
        sketch, column_rows, (((1,), (0,)), ((), ())), preferred_element_type=jnp.float32
    ).astype(jnp.bfloat16)
    right = jnp.concatenate([column_rows, projected], axis=0)

    pattern_col = lax.dynamic_index_in_dim(pattern, col_index, 1, keepdims=False)
    local_flags = lax.dynamic_slice_in_dim(pattern_col, row_index * slots, slots)
    info = jnp.concatenate([jnp.stack([z_index, core]), local_flags]).astype(jnp.int32)
    rows = order_rows(info, own, other)
    dense_out, sketch_out = final_update(info, rows, right, first_term, dense_tiles)
    return dense_out, sketch_out.reshape(1, rank_width, slots * tile_size)


def solution(mesh):
    in_specs = (
        P("row", "col", None),
        P(),
        P("row", "col"),
        P("col", None, "row"),
        P("row", None, "col"),
        P(None, "col"),
        P(),
        P(),
    )
    out_specs = (P("row", "col"), P("col", None, "row"))
    return jax.shard_map(
        on_device, mesh=mesh, in_specs=in_specs, out_specs=out_specs, check_vma=False
    )
```

time: 115 us -> 92.6 us (0.81)
  waiting for transfers between devices: 22.5 us -> 11.8 us
  starting transfers between devices: 52.3 us -> 45.6 us
  blocking collectives: 22.2 us -> 18.6 us
  local copies, waits for them, and re-layouts: 7.22 us -> 5.41 us
    all_to_all x1, waiting for transfers between devices: 10.7 us -> 0.01 us  [on_device(): parts = lax.all_to_all(parts, 'row', 0, 0)]
    all_to_all x1, starting transfers between devices: 8.67 us -> 4.85 us  [on_device(): lax.all_to_all(parts, 'col', 0, 0, axis_index_groups=same_core(z_count))]
    ppermute x4 -> x5, starting transfers between devices: 37 us -> 33.5 us  [shift(): return lax.ppermute(array, 'col', z_shift(z_count, up, down))]
    all_gather x1, blocking collectives: 9.05 us -> 5.54 us  [on_device(): lax.all_gather(parts, 'col', axis=1, axis_index_groups=same_chip(z_count))]
    all_to_all x1, waiting for transfers between devices: 6.2 us -> 4.41 us  [on_device(): lax.all_to_all(parts, 'col', 0, 0, axis_index_groups=same_core(z_count))]
    ppermute x1, starting transfers between devices: 2.26 us -> 3.58 us  [on_device(): other = lax.ppermute(own, 'col', core_swap(z_count))]
    reshape x1, local copies, waits for them, and re-layouts: 1.51 us -> 0.29 us  [on_device(): parts.reshape(halves, lane_blocks, col_count, HALF, LANES)]
    ppermute x4 -> x5, waiting for transfers between devices: 5.63 us -> 6.74 us  [shift(): return lax.ppermute(array, 'col', z_shift(z_count, up, down))]
  transfers between devices with their start and end apart: 7 -> 8, of which waited for: 4 -> 4; matrix products, arithmetic and copies ran while one was open for 7% -> 6% of each run, Pallas kernels for 1% -> 0%
where the time goes in v2:
time: 92.6 us; the launch traced here: 92 us
  starting transfers between devices  45.6 us (49%)
  blocking collectives  18.6 us (20%)
  waiting for transfers between devices  11.8 us (13%)
  Pallas kernels  6.18 us (7%)
  local copies, waits for them, and re-layouts  5.41 us (6%)
  matrix products  1.87 us (2%)
  other arithmetic  1.51 us (2%)
  between operations  0.95 us (1%)
    ppermute x5, starting transfers between devices, shift(): return lax.ppermute(array, 'col', z_shift(z_count, up, down))  33.5 us
    all_to_all x1, blocking collectives, on_device(): parts = lax.all_to_all(parts, 'row', 0, 0)  13.1 us
    ppermute x5, waiting for transfers between devices, shift(): return lax.ppermute(array, 'col', z_shift(z_count, up, down))  6.74 us
    all_gather x1, blocking collectives, on_device(): lax.all_gather(parts, 'col', axis=1, axis_index_groups=same_chip(z_count))  5.54 us
    all_to_all x1, starting transfers between devices, on_device(): lax.all_to_all(parts, 'col', 0, 0, axis_index_groups=same_core(z_count))  4.85 us
    all_to_all x1, waiting for transfers between devices, on_device(): lax.all_to_all(parts, 'col', 0, 0, axis_index_groups=same_core(z_count))  4.41 us
    all_to_all x1, starting transfers between devices, on_device(): parts = lax.all_to_all(parts, 'row', 0, 0)  3.66 us
    ppermute x1, starting transfers between devices, on_device(): other = lax.ppermute(own, 'col', core_swap(z_count))  3.58 us
  transfers between devices with their start and end apart: 8, of which 4 were waited for; matrix products, arithmetic and copies ran while one was open for 6% of the time, Pallas kernels for 0%

profile of v2, /device:TPU:1, one launch (start us, length us, event | category | flops | bytes accessed | tf_op | source)
XLA Modules:
  0.0 92.0 jit_solution(14721526208455986338)
XLA Ops:
  0.6 0.0 copy-start
  0.6 0.0 copy-start.3
  0.7 0.9 %copy.23 = bf16[2,2,2,8,512]{4,3,1,0,2:T(8,128)(2,1)S(1)} copy(bf16[2,2,2,8,512]{4,3,2,1,0:T(8,128)(2,1)} %bitcast.50) | data formatting | bytes 131072 | tf_op jit(solution)/shard_map/reshape | solution.py:203
  1.6 0.3 copy-done
  1.9 0.3 fusion.4
  2.2 0.1 copy.13
  2.3 16.3 %collective-permute-start = (bf16[1,2,16,1024]{3,2,1,0:T(8,128)(2,1)S(1)}, bf16[1,2,16,1024]{3,2,1,0:T(8,128)(2,1)S(1)}, u32[]{:S(2)}, u32[]{:S(2)}) collective-permute-start(bf16[1,2,16,1024]{3,2,1,0:T(8,128)(2,1)S(1)} %convert_element_type.28), channel_id=1, source_target_pairs={{0,256},{16,272},{32,288},{48,304},{64,320},{80,336},{96,352},{112... | collective-permute-start | bytes 196616 | tf_op jit(solution)/shard_map/ppermute | solution.py:38
  18.6 0.9 copy.14
  19.5 13.1 %all_to_all.15 = bf16[16,2,8,128]{3,2,1,0:T(8,128)(2,1)S(1)} all-to-all(bf16[16,2,8,128]{3,2,1,0:T(8,128)(2,1)S(1)} %bitcast.52), channel_id=1, replica_groups=mesh['col'=32,'row'=16] {'row'}, dimensions={0} | all-to-all | bytes 131072 | tf_op jit(solution)/shard_map/all_to_all | solution.py:198
  32.6 0.0 collective-permute-done._
  32.6 0.0 copy-done.3
  32.6 1.2 %select_tiles.1 = bf16[32,8,128]{2,1,0:T(8,128)(2,1)} custom-call(s32[32]{0:T(128)S(1)} %copy-done.3, bf16[32,8,128]{2,1,0:T(8,128)(2,1)S(1)} %bitcast.44, bf16[1,2,16,1024]{3,2,1,0:T(8,128)(2,1)S(1)} %collective-permute-done._), custom_call_target="tpu_custom_call" | custom-call | tf_op jit(solution)/shard_map/select_tiles/pallas_call | solution.py:91
  33.8 4.8 %all-to-all-start.1 = ((bf16[16,2,8,128]{3,2,1,0:T(8,128)(2,1)}), bf16[16,2,8,128]{3,2,1,0:T(8,128)(2,1)S(1)}, u32[]{:S(2)}, u32[]{:S(2)}) async-start(bf16[16,2,8,128]{3,2,1,0:T(8,128)(2,1)} %bitcast.10), calls=%async_computation.1 | async-start | bytes 131072 | tf_op jit(solution)/shard_map/all_to_all | solution.py:213
  38.6 7.2 %collective-permute-start.1 = (bf16[2,2,16,1024]{3,2,1,0:T(8,128)(2,1)S(1)}, bf16[2,2,16,1024]{3,2,1,0:T(8,128)(2,1)S(1)}, u32[]{:S(2)}, u32[]{:S(2)}) collective-permute-start(bf16[2,2,16,1024]{3,2,1,0:T(8,128)(2,1)S(1)} %constant_dynamic-update-slice_fusion.refs_0_), channel_id=1, source_target_pairs={{0,128},{16,400},{32,160},{48,432},{64,192},{80,464},{96,224},{112... | collective-permute-start | bytes 393224 | tf_op jit(solution)/shard_map/ppermute | solution.py:38
  45.8 4.4 %all-to-all-done.1.refs_2_ = bf16[16,2,8,128]{3,2,1,0:T(8,128)(2,1)S(1)} async-done(((bf16[16,2,8,128]{3,2,1,0:T(8,128)(2,1)}), bf16[16,2,8,128]{3,2,1,0:T(8,128)(2,1)S(1)}, u32[]{:S(2)}, u32[]{:S(2)}) %all-to-all-start.1) | async-done | bytes 65568 | tf_op jit(solution)/shard_map/all_to_all | solution.py:213
  50.3 5.5 %all-gather = bf16[16,4,8,128]{3,2,1,0:T(8,128)(2,1)S(1)} all-gather(bf16[16,2,8,128]{3,2,1,0:T(8,128)(2,1)S(1)} %all-to-all-done.1.refs_2_), channel_id=2, replica_groups={{0,16},{32,48},{64,80},{96,112},{128,144},{160,176},{192,208},{224,240}..., dimensions={1}, use_global_device_ids=true | all-gather | bytes 196608 | tf_op jit(solution)/shard_map/all_gather | solution.py:215
  55.8 0.0 copy-start.7
  55.8 0.0 collective-permute-done.1.refs_1_
  55.8 0.0 copy-start.1
  55.8 0.0 copy-start.4
  55.9 1.2 %broadcast_in_dim.8 = bf16[16,32,8,128]{3,2,1,0:T(8,128)(2,1)} broadcast(bf16[32,8,128]{2,1,0:T(8,128)(2,1)S(1)} %bitcast.48), dimensions={1,2,3} | broadcast | bytes 1114112 | tf_op jit(solution)/shard_map/broadcast_in_dim | solution.py:219
  57.1 3.7 %all-to-all-start.2 = ((bf16[16,32,8,128]{3,2,1,0:T(8,128)(2,1)}), bf16[16,32,8,128]{3,2,1,0:T(8,128)(2,1)S(1)}, u32[]{:S(2)}, u32[]{:S(2)}) async-start(bf16[16,32,8,128]{3,2,1,0:T(8,128)(2,1)} %broadcast_in_dim.8), calls=%async_computation.2 | async-start | bytes 2097152 | tf_op jit(solution)/shard_map/all_to_all | solution.py:224
  60.7 4.8 %collective-permute-start.4 = (bf16[4,2,16,1024]{3,2,1,0:T(8,128)(2,1)S(1)}, bf16[4,2,16,1024]{3,2,1,0:T(8,128)(2,1)S(1)}, u32[]{:S(2)}, u32[]{:S(2)}) collective-permute-start(bf16[4,2,16,1024]{3,2,1,0:T(8,128)(2,1)S(1)} %stack_after.1.refs_1_), channel_id=1, source_target_pairs={{0,64},{16,464},{32,96},{48,496},{64,128},{80,16},{96,160},{112,48... | collective-permute-start | bytes 786440 | tf_op jit(solution)/shard_map/ppermute | solution.py:38
  65.5 2.1 %collective-permute-start.3 = (bf16[4,2,16,1024]{3,2,1,0:T(8,128)(2,1)S(1)}, bf16[4,2,16,1024]{3,2,1,0:T(8,128)(2,1)S(1)}, u32[]{:S(2)}, u32[]{:S(2)}) collective-permute-start(bf16[4,2,16,1024]{3,2,1,0:T(8,128)(2,1)S(1)} %stack_after.1.refs_1_), channel_id=1, source_target_pairs={{0,480},{16,496},{32,0},{48,16},{64,32},{80,48},{96,64},{112,80},{... | collective-permute-start | bytes 786440 | tf_op jit(solution)/shard_map/ppermute | solution.py:38
  67.6 3.2 %collective-permute-start.2 = (bf16[4,2,16,1024]{3,2,1,0:T(8,128)(2,1)S(1)}, bf16[4,2,16,1024]{3,2,1,0:T(8,128)(2,1)}, u32[]{:S(2)}, u32[]{:S(2)}) collective-permute-start(bf16[4,2,16,1024]{3,2,1,0:T(8,128)(2,1)S(1)} %stack_after.1.refs_1_), channel_id=1, source_target_pairs={{0,32},{16,48},{32,64},{48,80},{64,96},{80,112},{96,128},{112,144}... | collective-permute-start | bytes 786440 | tf_op jit(solution)/shard_map/ppermute | solution.py:38
  70.8 0.0 copy-done.7
  70.8 0.1 reshape_squeeze.3
  70.9 0.0 copy-done.4
  70.9 1.3 %convolution_bitcast_fusion = f32[2,8,8,512]{3,2,1,0:T(8,128)S(1)} fusion(bf16[2,64,512]{2,1,0:T(8,128)(2,1)} %param.12, bf16[64,2,512]{2,1,0:T(2,128)(2,1)S(1)} %reshape_squeeze.3, bf16[64,512]{1,0:T(8,128)(2,1)S(1)} %copy-done.4), kind=kOutput, calls=%fused_computation.1 | convolution fusion | flops 16785408 | bytes 589824 | tf_op jit(solution)/shard_map/ikl,kib->lib/dot_general | solution.py:229
  72.2 0.0 copy-done.1
  72.2 1.1 %collective-permute-done.4 = bf16[4,2,16,1024]{3,2,1,0:T(8,128)(2,1)S(1)} collective-permute-done((bf16[4,2,16,1024]{3,2,1,0:T(8,128)(2,1)S(1)}, bf16[4,2,16,1024]{3,2,1,0:T(8,128)(2,1)S(1)}, u32[]{:S(2)}, u32[]{:S(2)}) %collective-permute-start.4) | collective-permute-done | bytes 262176 | tf_op jit(solution)/shard_map/ppermute | solution.py:38
  73.4 5.6 %collective-permute-done.3 = bf16[4,2,16,1024]{3,2,1,0:T(8,128)(2,1)S(1)} collective-permute-done((bf16[4,2,16,1024]{3,2,1,0:T(8,128)(2,1)S(1)}, bf16[4,2,16,1024]{3,2,1,0:T(8,128)(2,1)S(1)}, u32[]{:S(2)}, u32[]{:S(2)}) %collective-permute-start.3) | collective-permute-done | bytes 262176 | tf_op jit(solution)/shard_map/ppermute | solution.py:38
  79.0 0.0 copy-done.5
  79.0 0.7 copy-done.6
  79.7 0.0 collective-permute-done.2
  79.7 1.3 %pad_maximum_fusion.1.refs_0_ = bf16[16,2,16,1024]{3,2,1,0:T(8,128)(2,1)S(1)} fusion(bf16[4,2,16,1024]{3,2,1,0:T(8,128)(2,1)} %copy-done.5, bf16[4,2,16,1024]{3,2,1,0:T(8,128)(2,1)} %copy-done.6, bf16[4,2,16,1024]{3,2,1,0:T(8,128)(2,1)} %collective-permute-done.2, bf16[4,2,16,1024]{3,2,1,0:T(8,128)(2,1)} %copy-done.1), kind=kLoop, calls=%fused_computation.5 | loop fusion | flops 1572864 | bytes 2097152 | tf_op jit(solution)/shard_map/concatenate | solution.py:222
  81.0 0.0 all-to-all-done.2.refs_1_
  81.0 3.6 %collective-permute-start.5 = (bf16[16,2,16,1024]{3,2,1,0:T(8,128)(2,1)S(1)}, bf16[16,2,16,1024]{3,2,1,0:T(8,128)(2,1)}, u32[]{:S(2)}, u32[]{:S(2)}) collective-permute-start(bf16[16,2,16,1024]{3,2,1,0:T(8,128)(2,1)S(1)} %hold.3.refs_1_), channel_id=1, source_target_pairs={{0,16},{16,0},{32,48},{48,32},{64,80},{80,64},{96,112},{112,96},{1... | collective-permute-start | bytes 3145736 | tf_op jit(solution)/shard_map/ppermute | solution.py:234
  84.6 0.9 dynamic-slice_reduce_fusion
  85.5 0.1 pad_add_fusion.refs_0_.info_ref
  85.6 0.3 copy.17
  85.9 0.3 fusion
  86.2 0.1 pad_maximum_fusion.right_ref
  86.3 0.0 copy-start.2
  86.3 0.7 collective-permute-done.5.refs_2_
  87.0 1.5 %order_rows.1.rows_ref = bf16[1024,1024]{1,0:T(8,128)(2,1)S(1)} custom-call(s32[4]{0:T(128)S(1)} %pad_add_fusion.refs_0_.info_ref, bf16[16,2,16,1024]{3,2,1,0:T(8,128)(2,1)S(1)} %hold.3.refs_1_, bf16[16,2,16,1024]{3,2,1,0:T(8,128)(2,1)} %collective-permute-done.5.refs_2_), custom_call_target="tpu_custom_call" | custom-call | tf_op jit(solution)/shard_map/order_rows/pallas_call | solution.py:123
  88.5 0.0 copy-done.2
  88.5 3.5 %final_update.1 = (bf16[1024,512]{1,0:T(8,128)(2,1)}, bf16[64,1024]{1,0:T(8,128)(2,1)}) custom-call(s32[4]{0:T(128)S(1)} %pad_add_fusion.refs_0_.info_ref, bf16[1024,1024]{1,0:T(8,128)(2,1)S(1)} %order_rows.1.rows_ref, bf16[576,1024]{1,0:T(8,128)(2,1)S(1)} %pad_maximum_fusion.right_ref, f32[64,1024]{1,0:T(8,128)S(1)} %bitcast.42, bf16[1024,512]{1,0:T(8,128)(2,1)S(1)} %copy-done.2), custom_call_target="tpu_custom_call" | custom-call | flops 1207959552 | bytes 6291456 | tf_op jit(solution)/shard_map/final_update/pallas_call | solution.py:154
  (11 shorter events, 0.1 us)
Async XLA Ops:
  0.6 1.3 %copy-start = (bf16[2,512,512]{2,1,0:T(8,128)(2,1)S(1)}, bf16[2,512,512]{2,1,0:T(8,128)(2,1)}, u32[]{:S(2)}) copy-start(bf16[2,512,512]{2,1,0:T(8,128)(2,1)} %param.9) | copy-start | bytes 3145732
  0.6 31.9 %copy-start.3 = (s32[32]{0:T(128)S(1)}, s32[32]{0:T(128)}, u32[]{:S(2)}) copy-start(s32[32]{0:T(128)} %colmap_ref.1) | copy-start | bytes 388
  2.3 30.2 %collective-permute-start = (bf16[1,2,16,1024]{3,2,1,0:T(8,128)(2,1)S(1)}, bf16[1,2,16,1024]{3,2,1,0:T(8,128)(2,1)S(1)}, u32[]{:S(2)}, u32[]{:S(2)}) collective-permute-start(bf16[1,2,16,1024]{3,2,1,0:T(8,128)(2,1)S(1)} %convert_element_type.28), channel_id=1, source_target_pairs={{0,256},{16,272},{32,288},{48,304},{64,320},{80,336},{96,352},{112... | collective-permute-start | bytes 196616 | tf_op jit(solution)/shard_map/ppermute | solution.py:38
  33.8 16.5 %all-to-all-start.1 = ((bf16[16,2,8,128]{3,2,1,0:T(8,128)(2,1)}), bf16[16,2,8,128]{3,2,1,0:T(8,128)(2,1)S(1)}, u32[]{:S(2)}, u32[]{:S(2)}) async-start(bf16[16,2,8,128]{3,2,1,0:T(8,128)(2,1)} %bitcast.10), calls=%async_computation.1 | async-start | bytes 131072 | tf_op jit(solution)/shard_map/all_to_all | solution.py:213
  38.6 17.2 %collective-permute-start.1 = (bf16[2,2,16,1024]{3,2,1,0:T(8,128)(2,1)S(1)}, bf16[2,2,16,1024]{3,2,1,0:T(8,128)(2,1)S(1)}, u32[]{:S(2)}, u32[]{:S(2)}) collective-permute-start(bf16[2,2,16,1024]{3,2,1,0:T(8,128)(2,1)S(1)} %constant_dynamic-update-slice_fusion.refs_0_), channel_id=1, source_target_pairs={{0,128},{16,400},{32,160},{48,432},{64,192},{80,464},{96,224},{112... | collective-permute-start | bytes 393224 | tf_op jit(solution)/shard_map/ppermute | solution.py:38
  55.8 15.0 %copy-start.7 = (bf16[1,64,1024]{2,1,0:T(8,128)(2,1)S(1)}, bf16[1,64,1024]{2,1,0:T(8,128)(2,1)}, u32[]{:S(2)}) copy-start(bf16[1,64,1024]{2,1,0:T(8,128)(2,1)} %param.11) | copy-start | bytes 393220
  55.8 16.4 %copy-start.1 = (bf16[4,2,16,1024]{3,2,1,0:T(8,128)(2,1)}, bf16[4,2,16,1024]{3,2,1,0:T(8,128)(2,1)S(1)}, u32[]{:S(2)}) copy-start(bf16[4,2,16,1024]{3,2,1,0:T(8,128)(2,1)S(1)} %stack_after.1.refs_1_) | copy-start | bytes 786436
  55.8 15.1 %copy-start.4 = (bf16[64,512]{1,0:T(8,128)(2,1)S(1)}, bf16[64,512]{1,0:T(8,128)(2,1)}, u32[]{:S(2)}) copy-start(bf16[64,512]{1,0:T(8,128)(2,1)} %param.13) | copy-start | bytes 196612
  57.1 23.9 %all-to-all-start.2 = ((bf16[16,32,8,128]{3,2,1,0:T(8,128)(2,1)}), bf16[16,32,8,128]{3,2,1,0:T(8,128)(2,1)S(1)}, u32[]{:S(2)}, u32[]{:S(2)}) async-start(bf16[16,32,8,128]{3,2,1,0:T(8,128)(2,1)} %broadcast_in_dim.8), calls=%async_computation.2 | async-start | bytes 2097152 | tf_op jit(solution)/shard_map/all_to_all | solution.py:224
  60.7 12.6 %collective-permute-start.4 = (bf16[4,2,16,1024]{3,2,1,0:T(8,128)(2,1)S(1)}, bf16[4,2,16,1024]{3,2,1,0:T(8,128)(2,1)S(1)}, u32[]{:S(2)}, u32[]{:S(2)}) collective-permute-start(bf16[4,2,16,1024]{3,2,1,0:T(8,128)(2,1)S(1)} %stack_after.1.refs_1_), channel_id=1, source_target_pairs={{0,64},{16,464},{32,96},{48,496},{64,128},{80,16},{96,160},{112,48... | collective-permute-start | bytes 786440 | tf_op jit(solution)/shard_map/ppermute | solution.py:38
  65.5 13.5 %collective-permute-start.3 = (bf16[4,2,16,1024]{3,2,1,0:T(8,128)(2,1)S(1)}, bf16[4,2,16,1024]{3,2,1,0:T(8,128)(2,1)S(1)}, u32[]{:S(2)}, u32[]{:S(2)}) collective-permute-start(bf16[4,2,16,1024]{3,2,1,0:T(8,128)(2,1)S(1)} %stack_after.1.refs_1_), channel_id=1, source_target_pairs={{0,480},{16,496},{32,0},{48,16},{64,32},{80,48},{96,64},{112,80},{... | collective-permute-start | bytes 786440 | tf_op jit(solution)/shard_map/ppermute | solution.py:38
  67.6 12.1 %collective-permute-start.2 = (bf16[4,2,16,1024]{3,2,1,0:T(8,128)(2,1)S(1)}, bf16[4,2,16,1024]{3,2,1,0:T(8,128)(2,1)}, u32[]{:S(2)}, u32[]{:S(2)}) collective-permute-start(bf16[4,2,16,1024]{3,2,1,0:T(8,128)(2,1)S(1)} %stack_after.1.refs_1_), channel_id=1, source_target_pairs={{0,32},{16,48},{32,64},{48,80},{64,96},{80,112},{96,128},{112,144}... | collective-permute-start | bytes 786440 | tf_op jit(solution)/shard_map/ppermute | solution.py:38
  73.4 5.6 %copy-start.5 = (bf16[4,2,16,1024]{3,2,1,0:T(8,128)(2,1)}, bf16[4,2,16,1024]{3,2,1,0:T(8,128)(2,1)S(1)}, u32[]{:S(2)}) copy-start(bf16[4,2,16,1024]{3,2,1,0:T(8,128)(2,1)S(1)} %collective-permute-done.4) | copy-start | bytes 786436
  79.0 0.7 copy-start.6
  81.0 6.0 %collective-permute-start.5 = (bf16[16,2,16,1024]{3,2,1,0:T(8,128)(2,1)S(1)}, bf16[16,2,16,1024]{3,2,1,0:T(8,128)(2,1)}, u32[]{:S(2)}, u32[]{:S(2)}) collective-permute-start(bf16[16,2,16,1024]{3,2,1,0:T(8,128)(2,1)S(1)} %hold.3.refs_1_), channel_id=1, source_target_pairs={{0,16},{16,0},{32,48},{48,32},{64,80},{80,64},{96,112},{112,96},{1... | collective-permute-start | bytes 3145736 | tf_op jit(solution)/shard_map/ppermute | solution.py:234
  86.3 2.2 %copy-start.2 = (bf16[1024,512]{1,0:T(8,128)(2,1)S(1)}, bf16[1024,512]{1,0:T(8,128)(2,1)}, u32[]{:S(2)}) copy-start(bf16[1024,512]{1,0:T(8,128)(2,1)} %tiles_ref.1) | copy-start | bytes 3145732

commit v3 on v2

--- a/solution.py
+++ b/solution.py
@@ -38,13 +38,12 @@
     return lax.ppermute(array, "col", z_shift(z_count, up, down))
 
 
-def chunk_offsets(z_count):
+def far_offsets(z_count):
     half, quarter = z_count // 2, z_count // 4
-    return [
-        (near[0] + far[0], near[1] + far[1])
-        for near in ((0, 0), (-1, 0), (1, 0), (0, 2))
-        for far in ((0, 0), (half, 0), (0, quarter), (half, quarter))
-    ]
+    return ((0, 0), (half, 0), (0, quarter), (half, quarter))
+
+
+NEAR_OFFSETS = ((0, 0), (-1, 0), (1, 0), (0, 2))
 
 
 def stack_kernel(*refs):
@@ -82,6 +81,27 @@
     )(array, *earlier)
 
 
+def low_rank_kernel(left_ref, right_ref, sketch_ref, _, out_ref):
+    slots, _, tile_size = right_ref.shape
+    for slot in range(slots):
+        columns = slice(slot * tile_size, (slot + 1) * tile_size)
+        inner = lax.dot_general(
+            sketch_ref[...], right_ref[slot], (((1,), (1,)), ((), ())), preferred_element_type=jnp.float32
+        ).astype(left_ref.dtype)
+        out_ref[:, columns] = jnp.dot(inner, left_ref[:, columns], preferred_element_type=jnp.float32)
+
+
+def low_rank_term(left, right, sketch, earlier):
+    return pl.pallas_call(
+        low_rank_kernel,
+        out_shape=jax.ShapeDtypeStruct(left.shape, jnp.float32),
+        in_specs=[VMEM, VMEM, VMEM, ANY],
+        out_specs=VMEM,
+        compiler_params=pltpu.CompilerParams(vmem_limit_bytes=2 * 1024 * 1024),
+        name="low_rank_term",
+    )(left, right, sketch, earlier)
+
+
 def select_kernel(colmap_ref, tiles_ref, _, out_ref):
     for j in range(out_ref.shape[0]):
         out_ref[j] = tiles_ref[colmap_ref[j]]
@@ -98,46 +118,62 @@
     )(colmap, tiles, earlier)
 
 
-def order_kernel(offsets, info_ref, own_ref, other_ref, rows_ref):
-    z_count = len(offsets)
-    _, slots, piece, _ = own_ref.shape
-    tile_size = z_count * CORES * piece
-    z_index = info_ref[0]
-    core = info_ref[1]
-    for owner, chunk_ref in ((core, own_ref), (1 - core, other_ref)):
-        sign = 2 * owner - 1
-        for j, (fixed, mirrored) in enumerate(offsets):
-            z_from = (z_index + fixed + sign * mirrored + z_count) & (z_count - 1)
-            start = (z_from * CORES + owner) * piece
-            for slot in range(slots):
-                row = pl.multiple_of(slot * tile_size + start, piece)
-                rows_ref[pl.ds(row, piece), :] = chunk_ref[j, slot]
-
-
-def order_rows(info, own, other):
-    z_count, slots, piece, depth = own.shape
-
-    def kernel(*refs):
-        order_kernel(chunk_offsets(z_count), *refs)
-
-    return pl.pallas_call(
-        kernel,
-        out_shape=jax.ShapeDtypeStruct((CORES * z_count * slots * piece, depth), own.dtype),
-        in_specs=[SMEM, VMEM, VMEM],
+def place(z_index, owner, near, chunk_ref, rows_ref):
+    per_piece, slots, piece, _ = chunk_ref.shape
+    z_count = rows_ref.shape[0] // (slots * piece * CORES)
+    sign = 2 * owner - 1
+    for j, far in enumerate(far_offsets(z_count)):
+        fixed, mirrored = near[0] + far[0], near[1] + far[1]
+        z_from = (z_index + fixed + sign * mirrored + z_count) & (z_count - 1)
+        start = (z_from * CORES + owner) * piece
+        for slot in range(slots):
+            row = pl.multiple_of(slot * z_count * CORES * piece + start, piece)
+            rows_ref[pl.ds(row, piece), :] = chunk_ref[j, slot]
+
+
+def position():
+    col_index = lax.axis_index("col")
+    return col_index // CORES, col_index % CORES
+
+
+def order_kernel(*refs):
+    *chunk_refs, rows_ref = refs
+    z_index, core = position()
+    for near, chunk_ref in zip(NEAR_OFFSETS, chunk_refs[:4]):
+        place(z_index, core, near, chunk_ref, rows_ref)
+    for near, chunk_ref in zip(NEAR_OFFSETS, chunk_refs[4:]):
+        place(z_index, 1 - core, near, chunk_ref, rows_ref)
+
+
+def order_rows(own, other):
+    per_piece, slots, piece, depth = own[0].shape
+    count = len(own) * per_piece * CORES * slots * piece
+    return pl.pallas_call(
+        order_kernel,
+        out_shape=jax.ShapeDtypeStruct((count, depth), own[0].dtype),
+        in_specs=[VMEM] * (len(own) + len(other)),
         out_specs=VMEM,
         compiler_params=pltpu.CompilerParams(vmem_limit_bytes=6 * 1024 * 1024),
         name="order_rows",
-    )(info, own, other)
+    )(*own, *other)
 
 
 def final_kernel(
-    info_ref, rows_ref, right_ref, first_ref, tiles_ref, dense_ref, sketched_ref
+    pattern_ref, _, last_ref, right_ref, first_ref, tiles_ref, dense_ref, sketched_ref, rows_ref
 ):
     i = pl.program_id(0)
     tile_size = dense_ref.shape[1]
-    low = info_ref[2 + i * rows_ref.shape[0] // tile_size] == 1
+    slots = rows_ref.shape[0] // tile_size
+    z_index, core = position()
+
+    @pl.when(i == 0)
+    def _():
+        place(z_index, 1 - core, NEAR_OFFSETS[-1], last_ref, rows_ref)
+
+    tile_row = lax.axis_index("row") * slots + i * ROW_STEP // tile_size
+    low = pattern_ref[tile_row, lax.axis_index("col")] == 1
     product = lax.dot_general(
-        rows_ref[...],
+        rows_ref[pl.ds(pl.multiple_of(i * ROW_STEP, ROW_STEP), ROW_STEP), :],
         right_ref[...],
         (((1,), (1,)), ((), ())),
         preferred_element_type=jnp.float32,
@@ -148,7 +184,7 @@
     sketched_ref[...] = jnp.where(low, sketched, 0.0).astype(sketched_ref.dtype)
 
 
-def final_update(info, rows, right, first_term, dense_tiles):
+def final_update(pattern, rows, last, right, first_term, dense_tiles):
     count, depth = rows.shape
     rank_width, tile_size = first_term.shape[0], dense_tiles.shape[1]
     return pl.pallas_call(
@@ -157,10 +193,12 @@
         out_shape=(
             jax.ShapeDtypeStruct(dense_tiles.shape, dense_tiles.dtype),
             jax.ShapeDtypeStruct((rank_width, count), dense_tiles.dtype),
+            jax.ShapeDtypeStruct(rows.shape, rows.dtype),
         ),
         in_specs=[
             SMEM,
-            pl.BlockSpec((ROW_STEP, depth), lambda i: (i, 0)),
+            VMEM,
+            VMEM,
             VMEM,
             pl.BlockSpec((rank_width, ROW_STEP), lambda i: (0, i)),
             pl.BlockSpec((ROW_STEP, tile_size), lambda i: (i, 0)),
@@ -168,7 +206,9 @@
         out_specs=(
             pl.BlockSpec((ROW_STEP, tile_size), lambda i: (i, 0)),
             pl.BlockSpec((rank_width, ROW_STEP), lambda i: (0, i)),
+            VMEM,
         ),
+        input_output_aliases={1: 2},
         compiler_params=pltpu.CompilerParams(vmem_limit_bytes=12 * 1024 * 1024),
         cost_estimate=pl.CostEstimate(
             flops=2 * count * depth * (tile_size + rank_width),
@@ -176,7 +216,7 @@
             transcendentals=0,
         ),
         name="final_update",
-    )(info, rows, right, first_term, dense_tiles)
+    )(pattern, rows, last, right, first_term, dense_tiles)
 
 
 def on_device(panel, dblocks, dense_tiles, left_factor, right_factor, sketch, pattern, colmap):
@@ -187,8 +227,6 @@
     z_count = col_count // CORES
     row_count = pattern.shape[0] // slots
     col_index = lax.axis_index("col")
-    row_index = lax.axis_index("row")
-    z_index = col_index // CORES
     core = col_index % CORES
 
     lane_blocks = depth // LANES
@@ -207,31 +245,24 @@
     own = scaled.reshape(1, slots, piece, depth).astype(jnp.bfloat16)
     half = shift(own, z_count, z_count // 2, z_count // 2)
     parts = select_tiles(parts, colmap, half)
+    first_term = low_rank_term(left_factor[0], right_factor, sketch, parts)
     own = jnp.concatenate([own, half], axis=0)
     quarter = shift(own, z_count, z_count // 4, -(z_count // 4))
     parts = parts.reshape(z_count, CORES, HALF, LANES)
     parts = lax.all_to_all(parts, "col", 0, 0, axis_index_groups=same_core(z_count))
     own = stack_after([own, quarter], parts)
     parts = lax.all_gather(parts, "col", axis=1, axis_index_groups=same_chip(z_count))
-    parts = hold(parts, own)
+    parts = hold(parts, own, first_term)
     parts = lax.dynamic_index_in_dim(parts, core, 2, keepdims=False)
     parts = parts.reshape(1, col_count, HALF, LANES)
     parts = jnp.broadcast_to(parts, (row_count, col_count, HALF, LANES))
 
-    near = [shift(own, z_count, up, down) for up, down in ((1, 1), (-1, -1), (2, -2))]
-    own = jnp.concatenate([own] + near, axis=0)
+    own = [own] + [shift(own, z_count, up, down) for up, down in ((1, 1), (-1, -1), (2, -2))]
+    other = [lax.ppermute(part, "col", core_swap(z_count)) for part in own[:-1]]
 
     parts = lax.all_to_all(parts, "row", 0, 0)
-    inner_prod = jnp.einsum(
-        "ikb,lb->ikl", right_factor, sketch, preferred_element_type=jnp.float32
-    ).astype(jnp.bfloat16)
-    left_bases = left_factor[0].reshape(rank_width, slots, tile_size)
-    first_term = jnp.einsum(
-        "ikl,kib->lib", inner_prod, left_bases, preferred_element_type=jnp.float32
-    ).reshape(rank_width, slots * tile_size)
-
-    own = hold(own, parts, first_term)
-    other = lax.ppermute(own, "col", core_swap(z_count))
+    own[-1] = hold(own[-1], parts)
+    last = lax.ppermute(own[-1], "col", core_swap(z_count))
     parts = parts.reshape(halves, lane_blocks, col_count, HALF, LANES).transpose(2, 0, 3, 1, 4)
     column_rows = parts.reshape(tile_size, depth)
     projected = lax.dot_general(
@@ -239,11 +270,8 @@
     ).astype(jnp.bfloat16)
     right = jnp.concatenate([column_rows, projected], axis=0)
 
-    pattern_col = lax.dynamic_index_in_dim(pattern, col_index, 1, keepdims=False)
-    local_flags = lax.dynamic_slice_in_dim(pattern_col, row_index * slots, slots)
-    info = jnp.concatenate([jnp.stack([z_index, core]), local_flags]).astype(jnp.int32)
-    rows = order_rows(info, own, other)
-    dense_out, sketch_out = final_update(info, rows, right, first_term, dense_tiles)
+    rows = order_rows(own, other)
+    dense_out, sketch_out, _ = final_update(pattern, rows, last, right, first_term, dense_tiles)
     return dense_out, sketch_out.reshape(1, rank_width, slots * tile_size)
 
 

time: 92.6 us -> 91.6 us (0.989)
  starting transfers between devices: 45.6 us -> 55.2 us
  waiting for transfers between devices: 11.8 us -> 3.95 us
  other arithmetic: 1.51 us -> 0.11 us
  matrix products: 1.87 us -> 0.58 us
    ppermute x1 -> x4, starting transfers between devices: 3.58 us -> 13.1 us  [the longest x3 11.2 us: on_device(): other = [lax.ppermute(part, 'col', core_swap(z_count)) for part in own[:-1]]]
    ppermute x5, waiting for transfers between devices: 6.74 us -> 0.01 us  [shift(): return lax.ppermute(array, 'col', z_shift(z_count, up, down))]
    concatenate x2 -> x0, other arithmetic: 1.4 us -> none  [the longest x1 1.32 us: on_device(): own = jnp.concatenate([own] + near, axis=0)]
    dot_general x1 -> x0, matrix products: 1.3 us -> none  [on_device(): jnp.einsum('ikl,kib->lib', inner_prod, left_bases, preferred_element_type...]
  transfers between devices with their start and end apart: 8 -> 11, of which waited for: 4 -> 1; matrix products, arithmetic and copies ran while one was open for 6% -> 2% of each run, Pallas kernels for 0% -> 2%
where the time goes in v3:
time: 91.6 us; the launch traced here: 90.9 us
  starting transfers between devices  55.2 us (60%)
  blocking collectives  18.6 us (20%)
  Pallas kernels  6.74 us (7%)
  local copies, waits for them, and re-layouts  4.8 us (5%)
  waiting for transfers between devices  3.95 us (4%)
  between operations  0.98 us (1%)
    ppermute x5, starting transfers between devices, shift(): return lax.ppermute(array, 'col', z_shift(z_count, up, down))  33.5 us
    all_to_all x1, blocking collectives, on_device(): parts = lax.all_to_all(parts, 'row', 0, 0)  13.1 us
    ppermute x3, starting transfers between devices, on_device(): other = [lax.ppermute(part, 'col', core_swap(z_count)) for part in own[:-1]]  11.2 us
    all_gather x1, blocking collectives, on_device(): lax.all_gather(parts, 'col', axis=1, axis_index_groups=same_chip(z_count))  5.54 us
    all_to_all x1, starting transfers between devices, on_device(): lax.all_to_all(parts, 'col', 0, 0, axis_index_groups=same_core(z_count))  4.85 us
    all_to_all x1, waiting for transfers between devices, on_device(): lax.all_to_all(parts, 'col', 0, 0, axis_index_groups=same_core(z_count))  3.93 us
    pallas_call x1, Pallas kernels, final_update(): pl.pallas_call(final_kernel, grid=(count // ROW_STEP,), out_shape=(jax.Sh...  3.82 us
    all_to_all x1, starting transfers between devices, on_device(): parts = lax.all_to_all(parts, 'row', 0, 0)  3.66 us
  transfers between devices with their start and end apart: 11, of which 1 were waited for; matrix products, arithmetic and copies ran while one was open for 2% of the time, Pallas kernels for 2%

profile of v3, /device:TPU:1, one launch (start us, length us, event | category | flops | bytes accessed | tf_op | source)
XLA Modules:
  0.0 90.9 jit_solution(14475639520643137688)
XLA Ops:
  0.6 0.0 copy-start
  0.6 0.0 copy-start.6
  0.7 0.0 copy-start.2
  0.7 0.0 copy-start.4
  0.7 0.0 copy-start.3
  0.7 0.9 %copy.19 = bf16[2,2,2,8,512]{4,3,1,0,2:T(8,128)(2,1)S(1)} copy(bf16[2,2,2,8,512]{4,3,2,1,0:T(8,128)(2,1)} %bitcast.39) | data formatting | bytes 131072 | tf_op jit(solution)/shard_map/reshape | solution.py:241
  1.6 0.3 copy-done
  1.9 0.3 fusion.1
  2.2 0.1 copy.14
  2.3 16.3 %collective-permute-start = (bf16[1,2,16,1024]{3,2,1,0:T(8,128)(2,1)S(1)}, bf16[1,2,16,1024]{3,2,1,0:T(8,128)(2,1)S(1)}, u32[]{:S(2)}, u32[]{:S(2)}) collective-permute-start(bf16[1,2,16,1024]{3,2,1,0:T(8,128)(2,1)S(1)} %convert_element_type.25), channel_id=1, source_target_pairs={{0,256},{16,272},{32,288},{48,304},{64,320},{80,336},{96,352},{112... | collective-permute-start | bytes 196616 | tf_op jit(solution)/shard_map/ppermute | solution.py:38
  18.6 0.9 copy.15
  19.5 13.1 %all_to_all.15 = bf16[16,2,8,128]{3,2,1,0:T(8,128)(2,1)S(1)} all-to-all(bf16[16,2,8,128]{3,2,1,0:T(8,128)(2,1)S(1)} %bitcast.41), channel_id=1, replica_groups=mesh['col'=32,'row'=16] {'row'}, dimensions={0} | all-to-all | bytes 131072 | tf_op jit(solution)/shard_map/all_to_all | solution.py:236
  32.6 0.0 collective-permute-done._
  32.6 0.0 copy-done.6
  32.6 1.2 %select_tiles.1._ = bf16[32,8,128]{2,1,0:T(8,128)(2,1)} custom-call(s32[32]{0:T(128)S(1)} %copy-done.6, bf16[32,8,128]{2,1,0:T(8,128)(2,1)S(1)} %bitcast.32, bf16[1,2,16,1024]{3,2,1,0:T(8,128)(2,1)S(1)} %collective-permute-done._), custom_call_target="tpu_custom_call" | custom-call | tf_op jit(solution)/shard_map/select_tiles/pallas_call | solution.py:111
  33.8 4.8 %all-to-all-start.1 = ((bf16[16,2,8,128]{3,2,1,0:T(8,128)(2,1)}), bf16[16,2,8,128]{3,2,1,0:T(8,128)(2,1)S(1)}, u32[]{:S(2)}, u32[]{:S(2)}) async-start(bf16[16,2,8,128]{3,2,1,0:T(8,128)(2,1)} %bitcast.8), calls=%async_computation.1 | async-start | bytes 131072 | tf_op jit(solution)/shard_map/all_to_all | solution.py:252
  38.6 7.2 %collective-permute-start.1 = (bf16[2,2,16,1024]{3,2,1,0:T(8,128)(2,1)S(1)}, bf16[2,2,16,1024]{3,2,1,0:T(8,128)(2,1)S(1)}, u32[]{:S(2)}, u32[]{:S(2)}) collective-permute-start(bf16[2,2,16,1024]{3,2,1,0:T(8,128)(2,1)S(1)} %constant_dynamic-update-slice_fusion.refs_0_), channel_id=1, source_target_pairs={{0,128},{16,400},{32,160},{48,432},{64,192},{80,464},{96,224},{112... | collective-permute-start | bytes 393224 | tf_op jit(solution)/shard_map/ppermute | solution.py:38
  45.8 0.0 copy-done.2
  45.9 0.0 copy-done.4
  45.9 0.5 low_rank_term.1.refs_2_.first_ref
  46.3 3.9 %all-to-all-done.1.refs_2_ = bf16[16,2,8,128]{3,2,1,0:T(8,128)(2,1)S(1)} async-done(((bf16[16,2,8,128]{3,2,1,0:T(8,128)(2,1)}), bf16[16,2,8,128]{3,2,1,0:T(8,128)(2,1)S(1)}, u32[]{:S(2)}, u32[]{:S(2)}) %all-to-all-start.1) | async-done | bytes 65568 | tf_op jit(solution)/shard_map/all_to_all | solution.py:252
  50.3 5.5 %all-gather = bf16[16,4,8,128]{3,2,1,0:T(8,128)(2,1)S(1)} all-gather(bf16[16,2,8,128]{3,2,1,0:T(8,128)(2,1)S(1)} %all-to-all-done.1.refs_2_), channel_id=2, replica_groups={{0,16},{32,48},{64,80},{96,112},{128,144},{160,176},{192,208},{224,240}..., dimensions={1}, use_global_device_ids=true | all-gather | bytes 196608 | tf_op jit(solution)/shard_map/all_gather | solution.py:254
  55.8 0.0 collective-permute-done.1.refs_1_
  55.9 1.2 %broadcast_in_dim.8 = bf16[16,32,8,128]{3,2,1,0:T(8,128)(2,1)} broadcast(bf16[32,8,128]{2,1,0:T(8,128)(2,1)S(1)} %bitcast.37), dimensions={1,2,3} | broadcast | bytes 1114112 | tf_op jit(solution)/shard_map/broadcast_in_dim | solution.py:258
  57.0 3.7 %all-to-all-start.2 = ((bf16[16,32,8,128]{3,2,1,0:T(8,128)(2,1)}), bf16[16,32,8,128]{3,2,1,0:T(8,128)(2,1)S(1)}, u32[]{:S(2)}, u32[]{:S(2)}) async-start(bf16[16,32,8,128]{3,2,1,0:T(8,128)(2,1)} %broadcast_in_dim.8), calls=%async_computation.2 | async-start | bytes 2097152 | tf_op jit(solution)/shard_map/all_to_all | solution.py:263
  60.7 4.8 %collective-permute-start.3 = (bf16[4,2,16,1024]{3,2,1,0:T(8,128)(2,1)S(1)}, bf16[4,2,16,1024]{3,2,1,0:T(8,128)(2,1)S(1)}, u32[]{:S(2)}, u32[]{:S(2)}) collective-permute-start(bf16[4,2,16,1024]{3,2,1,0:T(8,128)(2,1)S(1)} %stack_after.1.refs_1_.refs_0_), channel_id=1, source_target_pairs={{0,480},{16,496},{32,0},{48,16},{64,32},{80,48},{96,64},{112,80},{... | collective-permute-start | bytes 786440 | tf_op jit(solution)/shard_map/ppermute | solution.py:38
  65.5 2.9 %collective-permute-start.2 = (bf16[4,2,16,1024]{3,2,1,0:T(8,128)(2,1)S(1)}, bf16[4,2,16,1024]{3,2,1,0:T(8,128)(2,1)S(1)}, u32[]{:S(2)}, u32[]{:S(2)}) collective-permute-start(bf16[4,2,16,1024]{3,2,1,0:T(8,128)(2,1)S(1)} %stack_after.1.refs_1_.refs_0_), channel_id=1, source_target_pairs={{0,32},{16,48},{32,64},{48,80},{64,96},{80,112},{96,128},{112,144}... | collective-permute-start | bytes 786440 | tf_op jit(solution)/shard_map/ppermute | solution.py:38
  68.4 2.3 %collective-permute-start.4 = (bf16[4,2,16,1024]{3,2,1,0:T(8,128)(2,1)S(1)}, bf16[4,2,16,1024]{3,2,1,0:T(8,128)(2,1)S(1)}, u32[]{:S(2)}, u32[]{:S(2)}) collective-permute-start(bf16[4,2,16,1024]{3,2,1,0:T(8,128)(2,1)S(1)} %stack_after.1.refs_1_.refs_0_), channel_id=1, source_target_pairs={{0,64},{16,464},{32,96},{48,496},{64,128},{80,16},{96,160},{112,48... | collective-permute-start | bytes 786440 | tf_op jit(solution)/shard_map/ppermute | solution.py:38
  70.8 4.0 %collective-permute-start.5 = (bf16[4,2,16,1024]{3,2,1,0:T(8,128)(2,1)S(1)}, bf16[4,2,16,1024]{3,2,1,0:T(8,128)(2,1)}, u32[]{:S(2)}, u32[]{:S(2)}) collective-permute-start(bf16[4,2,16,1024]{3,2,1,0:T(8,128)(2,1)S(1)} %stack_after.1.refs_1_.refs_0_), channel_id=1, source_target_pairs={{0,16},{16,0},{32,48},{48,32},{64,80},{80,64},{96,112},{112,96},{1... | collective-permute-start | bytes 786440 | tf_op jit(solution)/shard_map/ppermute | solution.py:261
  74.7 0.0 collective-permute-done.3.refs_2_
  74.8 1.9 %collective-permute-start.7 = (bf16[4,2,16,1024]{3,2,1,0:T(8,128)(2,1)S(1)}, bf16[4,2,16,1024]{3,2,1,0:T(8,128)(2,1)}, u32[]{:S(2)}, u32[]{:S(2)}) collective-permute-start(bf16[4,2,16,1024]{3,2,1,0:T(8,128)(2,1)S(1)} %collective-permute-done.3.refs_2_), channel_id=1, source_target_pairs={{0,16},{16,0},{32,48},{48,32},{64,80},{80,64},{96,112},{112,96},{1... | collective-permute-start | bytes 786440 | tf_op jit(solution)/shard_map/ppermute | solution.py:261
  76.7 0.0 collective-permute-done.2.refs_1_
  76.7 5.3 %collective-permute-start.6 = (bf16[4,2,16,1024]{3,2,1,0:T(8,128)(2,1)S(1)}, bf16[4,2,16,1024]{3,2,1,0:T(8,128)(2,1)}, u32[]{:S(2)}, u32[]{:S(2)}) collective-permute-start(bf16[4,2,16,1024]{3,2,1,0:T(8,128)(2,1)S(1)} %collective-permute-done.2.refs_1_), channel_id=1, source_target_pairs={{0,16},{16,0},{32,48},{48,32},{64,80},{80,64},{96,112},{112,96},{1... | collective-permute-start | bytes 786440 | tf_op jit(solution)/shard_map/ppermute | solution.py:261
  82.0 0.0 all-to-all-done.2.refs_1_
  82.1 0.3 copy.16
  82.4 0.0 collective-permute-done.4.refs_0_
  82.4 1.9 %collective-permute-start.8 = (bf16[4,2,16,1024]{3,2,1,0:T(8,128)(2,1)S(1)}, bf16[4,2,16,1024]{3,2,1,0:T(8,128)(2,1)S(1)}, u32[]{:S(2)}, u32[]{:S(2)}) collective-permute-start(bf16[4,2,16,1024]{3,2,1,0:T(8,128)(2,1)S(1)} %hold.3.refs_3_), channel_id=1, source_target_pairs={{0,16},{16,0},{32,48},{48,32},{64,80},{80,64},{96,112},{112,96},{1... | collective-permute-start | bytes 786440 | tf_op jit(solution)/shard_map/ppermute | solution.py:265
  84.3 0.3 fusion
  84.6 0.0 collective-permute-done.5.refs_4_
  84.6 0.0 collective-permute-done.7.refs_6_
  84.6 0.0 collective-permute-done.6.refs_5_
  84.6 1.2 %order_rows.1._ = bf16[1024,1024]{1,0:T(8,128)(2,1)S(1)} custom-call(bf16[4,2,16,1024]{3,2,1,0:T(8,128)(2,1)S(1)} %stack_after.1.refs_1_.refs_0_, bf16[4,2,16,1024]{3,2,1,0:T(8,128)(2,1)S(1)} %collective-permute-done.2.refs_1_, bf16[4,2,16,1024]{3,2,1,0:T(8,128)(2,1)S(1)} %collective-permute-done.3.refs_2_, bf16[4,2,16,1024]{3,2,1,0:T(8,128)(2,1)S(1)} %hold.3.refs_3_, ...), custom_call_target="tpu_custom_call" | custom-call | tf_op jit(solution)/shard_map/order_rows/pallas_call | solution.py:151
  85.9 0.0 copy-start.1
  85.9 0.0 copy-start.5
  85.9 0.1 pad_maximum_fusion.right_ref
  86.0 0.0 collective-permute-done.8.last_ref
  86.0 1.1 %copy-done.1 = bf16[1024,512]{1,0:T(8,128)(2,1)S(1)} copy-done((bf16[1024,512]{1,0:T(8,128)(2,1)S(1)}, bf16[1024,512]{1,0:T(8,128)(2,1)}, u32[]{:S(2)}) %copy-start.1) | copy-done | bytes 1048600
  87.1 3.8 %final_update.1 = (bf16[1024,512]{1,0:T(8,128)(2,1)}, bf16[64,1024]{1,0:T(8,128)(2,1)}, bf16[1024,1024]{1,0:T(8,128)(2,1)S(1)}) custom-call(s32[32,32]{1,0:T(8,128)S(1)} %copy-done.5, bf16[1024,1024]{1,0:T(8,128)(2,1)S(1)} %order_rows.1._, bf16[4,2,16,1024]{3,2,1,0:T(8,128)(2,1)S(1)} %collective-permute-done.8.last_ref, ...), custom_call_target="tpu_custom_call", output_to_operand_aliasing={{2}: (1, {})} | custom-call | flops 1207959552 | bytes 6291456 | tf_op jit(solution)/shard_map/final_update/pallas_call | solution.py:190
  (10 shorter events, 0.1 us)
Async XLA Ops:
  0.6 1.3 %copy-start = (bf16[2,512,512]{2,1,0:T(8,128)(2,1)S(1)}, bf16[2,512,512]{2,1,0:T(8,128)(2,1)}, u32[]{:S(2)}) copy-start(bf16[2,512,512]{2,1,0:T(8,128)(2,1)} %param.9) | copy-start | bytes 3145732
  0.6 31.9 %copy-start.6 = (s32[32]{0:T(128)S(1)}, s32[32]{0:T(128)}, u32[]{:S(2)}) copy-start(s32[32]{0:T(128)} %colmap_ref.1) | copy-start | bytes 388
  0.7 45.2 %copy-start.2 = (bf16[64,512]{1,0:T(8,128)(2,1)S(1)}, bf16[64,512]{1,0:T(8,128)(2,1)}, u32[]{:S(2)}) copy-start(bf16[64,512]{1,0:T(8,128)(2,1)} %sketch_ref.1) | copy-start | bytes 196612
  0.7 45.2 %copy-start.4 = (bf16[2,64,512]{2,1,0:T(8,128)(2,1)S(1)}, bf16[2,64,512]{2,1,0:T(8,128)(2,1)}, u32[]{:S(2)}) copy-start(bf16[2,64,512]{2,1,0:T(8,128)(2,1)} %right_ref.1) | copy-start | bytes 393220
  0.7 45.2 %copy-start.3 = (bf16[1,64,1024]{2,1,0:T(8,128)(2,1)S(1)}, bf16[1,64,1024]{2,1,0:T(8,128)(2,1)}, u32[]{:S(2)}) copy-start(bf16[1,64,1024]{2,1,0:T(8,128)(2,1)} %param.11) | copy-start | bytes 393220
  2.3 30.2 %collective-permute-start = (bf16[1,2,16,1024]{3,2,1,0:T(8,128)(2,1)S(1)}, bf16[1,2,16,1024]{3,2,1,0:T(8,128)(2,1)S(1)}, u32[]{:S(2)}, u32[]{:S(2)}) collective-permute-start(bf16[1,2,16,1024]{3,2,1,0:T(8,128)(2,1)S(1)} %convert_element_type.25), channel_id=1, source_target_pairs={{0,256},{16,272},{32,288},{48,304},{64,320},{80,336},{96,352},{112... | collective-permute-start | bytes 196616 | tf_op jit(solution)/shard_map/ppermute | solution.py:38
  33.8 16.5 %all-to-all-start.1 = ((bf16[16,2,8,128]{3,2,1,0:T(8,128)(2,1)}), bf16[16,2,8,128]{3,2,1,0:T(8,128)(2,1)S(1)}, u32[]{:S(2)}, u32[]{:S(2)}) async-start(bf16[16,2,8,128]{3,2,1,0:T(8,128)(2,1)} %bitcast.8), calls=%async_computation.1 | async-start | bytes 131072 | tf_op jit(solution)/shard_map/all_to_all | solution.py:252
  38.6 17.2 %collective-permute-start.1 = (bf16[2,2,16,1024]{3,2,1,0:T(8,128)(2,1)S(1)}, bf16[2,2,16,1024]{3,2,1,0:T(8,128)(2,1)S(1)}, u32[]{:S(2)}, u32[]{:S(2)}) collective-permute-start(bf16[2,2,16,1024]{3,2,1,0:T(8,128)(2,1)S(1)} %constant_dynamic-update-slice_fusion.refs_0_), channel_id=1, source_target_pairs={{0,128},{16,400},{32,160},{48,432},{64,192},{80,464},{96,224},{112... | collective-permute-start | bytes 393224 | tf_op jit(solution)/shard_map/ppermute | solution.py:38
  57.0 25.0 %all-to-all-start.2 = ((bf16[16,32,8,128]{3,2,1,0:T(8,128)(2,1)}), bf16[16,32,8,128]{3,2,1,0:T(8,128)(2,1)S(1)}, u32[]{:S(2)}, u32[]{:S(2)}) async-start(bf16[16,32,8,128]{3,2,1,0:T(8,128)(2,1)} %broadcast_in_dim.8), calls=%async_computation.2 | async-start | bytes 2097152 | tf_op jit(solution)/shard_map/all_to_all | solution.py:263
  60.7 14.0 %collective-permute-start.3 = (bf16[4,2,16,1024]{3,2,1,0:T(8,128)(2,1)S(1)}, bf16[4,2,16,1024]{3,2,1,0:T(8,128)(2,1)S(1)}, u32[]{:S(2)}, u32[]{:S(2)}) collective-permute-start(bf16[4,2,16,1024]{3,2,1,0:T(8,128)(2,1)S(1)} %stack_after.1.refs_1_.refs_0_), channel_id=1, source_target_pairs={{0,480},{16,496},{32,0},{48,16},{64,32},{80,48},{96,64},{112,80},{... | collective-permute-start | bytes 786440 | tf_op jit(solution)/shard_map/ppermute | solution.py:38
  65.5 11.2 %collective-permute-start.2 = (bf16[4,2,16,1024]{3,2,1,0:T(8,128)(2,1)S(1)}, bf16[4,2,16,1024]{3,2,1,0:T(8,128)(2,1)S(1)}, u32[]{:S(2)}, u32[]{:S(2)}) collective-permute-start(bf16[4,2,16,1024]{3,2,1,0:T(8,128)(2,1)S(1)} %stack_after.1.refs_1_.refs_0_), channel_id=1, source_target_pairs={{0,32},{16,48},{32,64},{48,80},{64,96},{80,112},{96,128},{112,144}... | collective-permute-start | bytes 786440 | tf_op jit(solution)/shard_map/ppermute | solution.py:38
  68.4 13.9 %collective-permute-start.4 = (bf16[4,2,16,1024]{3,2,1,0:T(8,128)(2,1)S(1)}, bf16[4,2,16,1024]{3,2,1,0:T(8,128)(2,1)S(1)}, u32[]{:S(2)}, u32[]{:S(2)}) collective-permute-start(bf16[4,2,16,1024]{3,2,1,0:T(8,128)(2,1)S(1)} %stack_after.1.refs_1_.refs_0_), channel_id=1, source_target_pairs={{0,64},{16,464},{32,96},{48,496},{64,128},{80,16},{96,160},{112,48... | collective-permute-start | bytes 786440 | tf_op jit(solution)/shard_map/ppermute | solution.py:38
  70.8 13.8 %collective-permute-start.5 = (bf16[4,2,16,1024]{3,2,1,0:T(8,128)(2,1)S(1)}, bf16[4,2,16,1024]{3,2,1,0:T(8,128)(2,1)}, u32[]{:S(2)}, u32[]{:S(2)}) collective-permute-start(bf16[4,2,16,1024]{3,2,1,0:T(8,128)(2,1)S(1)} %stack_after.1.refs_1_.refs_0_), channel_id=1, source_target_pairs={{0,16},{16,0},{32,48},{48,32},{64,80},{80,64},{96,112},{112,96},{1... | collective-permute-start | bytes 786440 | tf_op jit(solution)/shard_map/ppermute | solution.py:261
  74.8 9.9 %collective-permute-start.7 = (bf16[4,2,16,1024]{3,2,1,0:T(8,128)(2,1)S(1)}, bf16[4,2,16,1024]{3,2,1,0:T(8,128)(2,1)}, u32[]{:S(2)}, u32[]{:S(2)}) collective-permute-start(bf16[4,2,16,1024]{3,2,1,0:T(8,128)(2,1)S(1)} %collective-permute-done.3.refs_2_), channel_id=1, source_target_pairs={{0,16},{16,0},{32,48},{48,32},{64,80},{80,64},{96,112},{112,96},{1... | collective-permute-start | bytes 786440 | tf_op jit(solution)/shard_map/ppermute | solution.py:261
  76.7 7.9 %collective-permute-start.6 = (bf16[4,2,16,1024]{3,2,1,0:T(8,128)(2,1)S(1)}, bf16[4,2,16,1024]{3,2,1,0:T(8,128)(2,1)}, u32[]{:S(2)}, u32[]{:S(2)}) collective-permute-start(bf16[4,2,16,1024]{3,2,1,0:T(8,128)(2,1)S(1)} %collective-permute-done.2.refs_1_), channel_id=1, source_target_pairs={{0,16},{16,0},{32,48},{48,32},{64,80},{80,64},{96,112},{112,96},{1... | collective-permute-start | bytes 786440 | tf_op jit(solution)/shard_map/ppermute | solution.py:261
  82.4 3.6 %collective-permute-start.8 = (bf16[4,2,16,1024]{3,2,1,0:T(8,128)(2,1)S(1)}, bf16[4,2,16,1024]{3,2,1,0:T(8,128)(2,1)S(1)}, u32[]{:S(2)}, u32[]{:S(2)}) collective-permute-start(bf16[4,2,16,1024]{3,2,1,0:T(8,128)(2,1)S(1)} %hold.3.refs_3_), channel_id=1, source_target_pairs={{0,16},{16,0},{32,48},{48,32},{64,80},{80,64},{96,112},{112,96},{1... | collective-permute-start | bytes 786440 | tf_op jit(solution)/shard_map/ppermute | solution.py:265
  85.9 1.2 %copy-start.1 = (bf16[1024,512]{1,0:T(8,128)(2,1)S(1)}, bf16[1024,512]{1,0:T(8,128)(2,1)}, u32[]{:S(2)}) copy-start(bf16[1024,512]{1,0:T(8,128)(2,1)} %tiles_ref.1) | copy-start | bytes 3145732
  85.9 1.2 %copy-start.5 = (s32[32,32]{1,0:T(8,128)S(1)}, s32[32,32]{1,0:T(8,128)}, u32[]{:S(2)}) copy-start(s32[32,32]{1,0:T(8,128)} %pattern_ref.1) | copy-start | bytes 12292

commit v4 on v3

--- a/solution.py
+++ b/solution.py
@@ -43,7 +43,7 @@
     return ((0, 0), (half, 0), (0, quarter), (half, quarter))
 
 
-NEAR_OFFSETS = ((0, 0), (-1, 0), (1, 0), (0, 2))
+NEAR_OFFSETS = (((0, 0),), ((-1, 0),), ((1, 0), (0, 2)))
 
 
 def stack_kernel(*refs):
@@ -65,8 +65,8 @@
     )(*chunks, earlier)
 
 
-def same_kernel(*refs):
-    pass
+def same_kernel(array_ref, *refs):
+    refs[-1][...] = array_ref[...]
 
 
 def hold(array, *earlier):
@@ -76,7 +76,7 @@
         in_specs=[VMEM] * (1 + len(earlier)),
         out_specs=VMEM,
         input_output_aliases={0: 0},
-        compiler_params=pltpu.CompilerParams(vmem_limit_bytes=1024 * 1024),
+        compiler_params=pltpu.CompilerParams(vmem_limit_bytes=4 * 1024 * 1024),
         name="hold",
     )(array, *earlier)
 
@@ -118,11 +118,12 @@
     )(colmap, tiles, earlier)
 
 
-def place(z_index, owner, near, chunk_ref, rows_ref):
-    per_piece, slots, piece, _ = chunk_ref.shape
+def place(z_index, owner, nears, chunk_ref, rows_ref):
+    _, slots, piece, _ = chunk_ref.shape
     z_count = rows_ref.shape[0] // (slots * piece * CORES)
     sign = 2 * owner - 1
-    for j, far in enumerate(far_offsets(z_count)):
+    offsets = [(near, far) for near in nears for far in far_offsets(z_count)]
+    for j, (near, far) in enumerate(offsets):
         fixed, mirrored = near[0] + far[0], near[1] + far[1]
         z_from = (z_index + fixed + sign * mirrored + z_count) & (z_count - 1)
         start = (z_from * CORES + owner) * piece
@@ -139,15 +140,15 @@
 def order_kernel(*refs):
     *chunk_refs, rows_ref = refs
     z_index, core = position()
-    for near, chunk_ref in zip(NEAR_OFFSETS, chunk_refs[:4]):
+    for near, chunk_ref in zip(NEAR_OFFSETS, chunk_refs[: len(NEAR_OFFSETS)]):
         place(z_index, core, near, chunk_ref, rows_ref)
-    for near, chunk_ref in zip(NEAR_OFFSETS, chunk_refs[4:]):
+    for near, chunk_ref in zip(NEAR_OFFSETS, chunk_refs[len(NEAR_OFFSETS) :]):
         place(z_index, 1 - core, near, chunk_ref, rows_ref)
 
 
 def order_rows(own, other):
-    per_piece, slots, piece, depth = own[0].shape
-    count = len(own) * per_piece * CORES * slots * piece
+    _, slots, piece, depth = own[0].shape
+    count = sum(part.shape[0] for part in own) * CORES * slots * piece
     return pl.pallas_call(
         order_kernel,
         out_shape=jax.ShapeDtypeStruct((count, depth), own[0].dtype),
@@ -159,7 +160,7 @@
 
 
 def final_kernel(
-    pattern_ref, _, last_ref, right_ref, first_ref, tiles_ref, dense_ref, sketched_ref, rows_ref
+    pattern_ref, rows_ref, last_ref, right_ref, first_ref, tiles_ref, dense_ref, sketched_ref, _
 ):
     i = pl.program_id(0)
     tile_size = dense_ref.shape[1]
@@ -257,11 +258,12 @@
     parts = parts.reshape(1, col_count, HALF, LANES)
     parts = jnp.broadcast_to(parts, (row_count, col_count, HALF, LANES))
 
-    own = [own] + [shift(own, z_count, up, down) for up, down in ((1, 1), (-1, -1), (2, -2))]
-    other = [lax.ppermute(part, "col", core_swap(z_count)) for part in own[:-1]]
+    near = [shift(own, z_count, up, down) for up, down in ((1, 1), (-1, -1), (2, -2))]
+    own = [own, near[0]]
+    other = [lax.ppermute(part, "col", core_swap(z_count)) for part in own]
 
     parts = lax.all_to_all(parts, "row", 0, 0)
-    own[-1] = hold(own[-1], parts)
+    own.append(hold(jnp.concatenate(near[1:], axis=0), parts))
     last = lax.ppermute(own[-1], "col", core_swap(z_count))
     parts = parts.reshape(halves, lane_blocks, col_count, HALF, LANES).transpose(2, 0, 3, 1, 4)
     column_rows = parts.reshape(tile_size, depth)

time: 91.6 us -> 91.2 us (level)
  starting transfers between devices: 55.2 us -> 51.9 us
  waiting for transfers between devices: 3.95 us -> 7.1 us
    ppermute x3 -> x2, starting transfers between devices: 11.2 us -> 7.09 us  [on_device(): other = [lax.ppermute(part, 'col', core_swap(z_count)) for part in own]]
    ppermute x5, waiting for transfers between devices: 0.01 us -> 3.17 us  [shift(): return lax.ppermute(array, 'col', z_shift(z_count, up, down))]
  transfers between devices with their start and end apart: 11 -> 10, of which waited for: 1 -> 2; matrix products, arithmetic and copies ran while one was open for 2% -> 2% of each run, Pallas kernels for 2% -> 2%
where the time goes in v4:
time: 91.2 us; the launch traced here: 90.6 us
  starting transfers between devices  51.9 us (57%)
  blocking collectives  18.6 us (20%)
  waiting for transfers between devices  7.1 us (8%)
  Pallas kernels  6.76 us (7%)
  local copies, waits for them, and re-layouts  4.48 us (5%)
  between operations  0.96 us (1%)
    ppermute x5, starting transfers between devices, shift(): return lax.ppermute(array, 'col', z_shift(z_count, up, down))  33.5 us
    all_to_all x1, blocking collectives, on_device(): parts = lax.all_to_all(parts, 'row', 0, 0)  13.1 us
    ppermute x2, starting transfers between devices, on_device(): other = [lax.ppermute(part, 'col', core_swap(z_count)) for part in own]  7.09 us
    all_gather x1, blocking collectives, on_device(): lax.all_gather(parts, 'col', axis=1, axis_index_groups=same_chip(z_count))  5.54 us
    all_to_all x1, starting transfers between devices, on_device(): lax.all_to_all(parts, 'col', 0, 0, axis_index_groups=same_core(z_count))  4.85 us
    all_to_all x1, waiting for transfers between devices, on_device(): lax.all_to_all(parts, 'col', 0, 0, axis_index_groups=same_core(z_count))  3.93 us
    pallas_call x1, Pallas kernels, final_update(): pl.pallas_call(final_kernel, grid=(count // ROW_STEP,), out_shape=(jax.Sh...  3.83 us
    all_to_all x1, starting transfers between devices, on_device(): parts = lax.all_to_all(parts, 'row', 0, 0)  3.66 us
  transfers between devices with their start and end apart: 10, of which 2 were waited for; matrix products, arithmetic and copies ran while one was open for 2% of the time, Pallas kernels for 2%

profile of v4, /device:TPU:1, one launch (start us, length us, event | category | flops | bytes accessed | tf_op | source)
XLA Modules:
  0.0 90.6 jit_solution(1512355094800649694)
XLA Ops:
  0.6 0.0 copy-start
  0.6 0.0 copy-start.6
  0.7 0.0 copy-start.2
  0.7 0.0 copy-start.4
  0.7 0.0 copy-start.3
  0.7 0.9 %copy.19 = bf16[2,2,2,8,512]{4,3,1,0,2:T(8,128)(2,1)S(1)} copy(bf16[2,2,2,8,512]{4,3,2,1,0:T(8,128)(2,1)} %bitcast.39) | data formatting | bytes 131072 | tf_op jit(solution)/shard_map/reshape | solution.py:242
  1.6 0.3 copy-done
  1.9 0.3 fusion.1
  2.2 0.1 copy.14
  2.3 16.3 %collective-permute-start = (bf16[1,2,16,1024]{3,2,1,0:T(8,128)(2,1)S(1)}, bf16[1,2,16,1024]{3,2,1,0:T(8,128)(2,1)S(1)}, u32[]{:S(2)}, u32[]{:S(2)}) collective-permute-start(bf16[1,2,16,1024]{3,2,1,0:T(8,128)(2,1)S(1)} %convert_element_type.25), channel_id=1, source_target_pairs={{0,256},{16,272},{32,288},{48,304},{64,320},{80,336},{96,352},{112... | collective-permute-start | bytes 196616 | tf_op jit(solution)/shard_map/ppermute | solution.py:38
  18.6 0.9 copy.15
  19.5 13.1 %all_to_all.15 = bf16[16,2,8,128]{3,2,1,0:T(8,128)(2,1)S(1)} all-to-all(bf16[16,2,8,128]{3,2,1,0:T(8,128)(2,1)S(1)} %bitcast.41), channel_id=1, replica_groups=mesh['col'=32,'row'=16] {'row'}, dimensions={0} | all-to-all | bytes 131072 | tf_op jit(solution)/shard_map/all_to_all | solution.py:237
  32.6 0.0 collective-permute-done._
  32.6 0.0 copy-done.6
  32.6 1.2 %select_tiles.1._ = bf16[32,8,128]{2,1,0:T(8,128)(2,1)} custom-call(s32[32]{0:T(128)S(1)} %copy-done.6, bf16[32,8,128]{2,1,0:T(8,128)(2,1)S(1)} %bitcast.32, bf16[1,2,16,1024]{3,2,1,0:T(8,128)(2,1)S(1)} %collective-permute-done._), custom_call_target="tpu_custom_call" | custom-call | tf_op jit(solution)/shard_map/select_tiles/pallas_call | solution.py:111
  33.8 4.8 %all-to-all-start.1 = ((bf16[16,2,8,128]{3,2,1,0:T(8,128)(2,1)}), bf16[16,2,8,128]{3,2,1,0:T(8,128)(2,1)S(1)}, u32[]{:S(2)}, u32[]{:S(2)}) async-start(bf16[16,2,8,128]{3,2,1,0:T(8,128)(2,1)} %bitcast.8), calls=%async_computation.1 | async-start | bytes 131072 | tf_op jit(solution)/shard_map/all_to_all | solution.py:253
  38.6 7.2 %collective-permute-start.1 = (bf16[2,2,16,1024]{3,2,1,0:T(8,128)(2,1)S(1)}, bf16[2,2,16,1024]{3,2,1,0:T(8,128)(2,1)S(1)}, u32[]{:S(2)}, u32[]{:S(2)}) collective-permute-start(bf16[2,2,16,1024]{3,2,1,0:T(8,128)(2,1)S(1)} %constant_dynamic-update-slice_fusion.refs_0_), channel_id=1, source_target_pairs={{0,128},{16,400},{32,160},{48,432},{64,192},{80,464},{96,224},{112... | collective-permute-start | bytes 393224 | tf_op jit(solution)/shard_map/ppermute | solution.py:38
  45.8 0.0 copy-done.2
  45.9 0.0 copy-done.4
  45.9 0.0 copy-done.3
  45.9 0.5 low_rank_term.1.refs_1_.first_ref
  46.3 3.9 %all-to-all-done.1.refs_2_ = bf16[16,2,8,128]{3,2,1,0:T(8,128)(2,1)S(1)} async-done(((bf16[16,2,8,128]{3,2,1,0:T(8,128)(2,1)}), bf16[16,2,8,128]{3,2,1,0:T(8,128)(2,1)S(1)}, u32[]{:S(2)}, u32[]{:S(2)}) %all-to-all-start.1) | async-done | bytes 65568 | tf_op jit(solution)/shard_map/all_to_all | solution.py:253
  50.3 5.5 %all-gather = bf16[16,4,8,128]{3,2,1,0:T(8,128)(2,1)S(1)} all-gather(bf16[16,2,8,128]{3,2,1,0:T(8,128)(2,1)S(1)} %all-to-all-done.1.refs_2_), channel_id=2, replica_groups={{0,16},{32,48},{64,80},{96,112},{128,144},{160,176},{192,208},{224,240}..., dimensions={1}, use_global_device_ids=true | all-gather | bytes 196608 | tf_op jit(solution)/shard_map/all_gather | solution.py:255
  55.8 0.0 collective-permute-done.1.refs_1_
  55.9 1.2 %broadcast_in_dim.8 = bf16[16,32,8,128]{3,2,1,0:T(8,128)(2,1)} broadcast(bf16[32,8,128]{2,1,0:T(8,128)(2,1)S(1)} %bitcast.37), dimensions={1,2,3} | broadcast | bytes 1114112 | tf_op jit(solution)/shard_map/broadcast_in_dim | solution.py:259
  57.1 3.7 %all-to-all-start.2 = ((bf16[16,32,8,128]{3,2,1,0:T(8,128)(2,1)}), bf16[16,32,8,128]{3,2,1,0:T(8,128)(2,1)S(1)}, u32[]{:S(2)}, u32[]{:S(2)}) async-start(bf16[16,32,8,128]{3,2,1,0:T(8,128)(2,1)} %broadcast_in_dim.8), calls=%async_computation.2 | async-start | bytes 2097152 | tf_op jit(solution)/shard_map/all_to_all | solution.py:265
  60.7 5.8 %collective-permute-start.2 = (bf16[4,2,16,1024]{3,2,1,0:T(8,128)(2,1)S(1)}, bf16[4,2,16,1024]{3,2,1,0:T(8,128)(2,1)S(1)}, u32[]{:S(2)}, u32[]{:S(2)}) collective-permute-start(bf16[4,2,16,1024]{3,2,1,0:T(8,128)(2,1)S(1)} %stack_after.1.refs_0_), channel_id=1, source_target_pairs={{0,32},{16,48},{32,64},{48,80},{64,96},{80,112},{96,128},{112,144}... | collective-permute-start | bytes 786440 | tf_op jit(solution)/shard_map/ppermute | solution.py:38
  66.6 2.1 %collective-permute-start.4 = (bf16[4,2,16,1024]{3,2,1,0:T(8,128)(2,1)S(1)}, bf16[4,2,16,1024]{3,2,1,0:T(8,128)(2,1)S(1)}, u32[]{:S(2)}, u32[]{:S(2)}) collective-permute-start(bf16[4,2,16,1024]{3,2,1,0:T(8,128)(2,1)S(1)} %stack_after.1.refs_0_), channel_id=1, source_target_pairs={{0,64},{16,464},{32,96},{48,496},{64,128},{80,16},{96,160},{112,48... | collective-permute-start | bytes 786440 | tf_op jit(solution)/shard_map/ppermute | solution.py:38
  68.6 2.2 %collective-permute-start.3 = (bf16[4,2,16,1024]{3,2,1,0:T(8,128)(2,1)S(1)}, bf16[4,2,16,1024]{3,2,1,0:T(8,128)(2,1)S(1)}, u32[]{:S(2)}, u32[]{:S(2)}) collective-permute-start(bf16[4,2,16,1024]{3,2,1,0:T(8,128)(2,1)S(1)} %stack_after.1.refs_0_), channel_id=1, source_target_pairs={{0,480},{16,496},{32,0},{48,16},{64,32},{80,48},{96,64},{112,80},{... | collective-permute-start | bytes 786440 | tf_op jit(solution)/shard_map/ppermute | solution.py:38
  70.8 5.2 %collective-permute-start.5 = (bf16[4,2,16,1024]{3,2,1,0:T(8,128)(2,1)S(1)}, bf16[4,2,16,1024]{3,2,1,0:T(8,128)(2,1)}, u32[]{:S(2)}, u32[]{:S(2)}) collective-permute-start(bf16[4,2,16,1024]{3,2,1,0:T(8,128)(2,1)S(1)} %stack_after.1.refs_0_), channel_id=1, source_target_pairs={{0,16},{16,0},{32,48},{48,32},{64,80},{80,64},{96,112},{112,96},{1... | collective-permute-start | bytes 786440 | tf_op jit(solution)/shard_map/ppermute | solution.py:263
  76.0 0.0 collective-permute-done.2.refs_1_
  76.0 1.9 %collective-permute-start.6 = (bf16[4,2,16,1024]{3,2,1,0:T(8,128)(2,1)S(1)}, bf16[4,2,16,1024]{3,2,1,0:T(8,128)(2,1)}, u32[]{:S(2)}, u32[]{:S(2)}) collective-permute-start(bf16[4,2,16,1024]{3,2,1,0:T(8,128)(2,1)S(1)} %collective-permute-done.2.refs_1_), channel_id=1, source_target_pairs={{0,16},{16,0},{32,48},{48,32},{64,80},{80,64},{96,112},{112,96},{1... | collective-permute-start | bytes 786440 | tf_op jit(solution)/shard_map/ppermute | solution.py:263
  77.9 0.0 collective-permute-done.4
  77.9 3.2 %collective-permute-done.3 = bf16[4,2,16,1024]{3,2,1,0:T(8,128)(2,1)S(1)} collective-permute-done((bf16[4,2,16,1024]{3,2,1,0:T(8,128)(2,1)S(1)}, bf16[4,2,16,1024]{3,2,1,0:T(8,128)(2,1)S(1)}, u32[]{:S(2)}, u32[]{:S(2)}) %collective-permute-start.3) | collective-permute-done | bytes 262176 | tf_op jit(solution)/shard_map/ppermute | solution.py:38
  81.1 0.0 all-to-all-done.2.refs_0_
  81.2 0.1 hold.3.refs_2_
  81.2 2.8 %collective-permute-start.7 = (bf16[8,2,16,1024]{3,2,1,0:T(8,128)(2,1)S(1)}, bf16[8,2,16,1024]{3,2,1,0:T(8,128)(2,1)S(1)}, u32[]{:S(2)}, u32[]{:S(2)}) collective-permute-start(bf16[8,2,16,1024]{3,2,1,0:T(8,128)(2,1)S(1)} %hold.3.refs_2_), channel_id=1, source_target_pairs={{0,16},{16,0},{32,48},{48,32},{64,80},{80,64},{96,112},{112,96},{1... | collective-permute-start | bytes 1572872 | tf_op jit(solution)/shard_map/ppermute | solution.py:267
  84.0 0.3 copy.16
  84.3 0.0 collective-permute-done.5.refs_3_
  84.3 0.0 collective-permute-done.6.refs_4_
  84.3 1.2 %order_rows.1.rows_ref = bf16[1024,1024]{1,0:T(8,128)(2,1)S(1)} custom-call(bf16[4,2,16,1024]{3,2,1,0:T(8,128)(2,1)S(1)} %stack_after.1.refs_0_, bf16[4,2,16,1024]{3,2,1,0:T(8,128)(2,1)S(1)} %collective-permute-done.2.refs_1_, bf16[8,2,16,1024]{3,2,1,0:T(8,128)(2,1)S(1)} %hold.3.refs_2_, bf16[4,2,16,1024]{3,2,1,0:T(8,128)(2,1)} %collective-permute-done.5.refs_3_, ...), custom_call_target="tpu_custom_call" | custom-call | tf_op jit(solution)/shard_map/order_rows/pallas_call | solution.py:152
  85.5 0.0 copy-start.1
  85.5 0.0 copy-start.5
  85.5 0.3 fusion
  85.8 0.1 pad_maximum_fusion.right_ref
  85.9 0.0 collective-permute-done.7.last_ref
  85.9 0.8 copy-done.1
  86.7 3.8 %final_update.1 = (bf16[1024,512]{1,0:T(8,128)(2,1)}, bf16[64,1024]{1,0:T(8,128)(2,1)}, bf16[1024,1024]{1,0:T(8,128)(2,1)S(1)}) custom-call(s32[32,32]{1,0:T(8,128)S(1)} %copy-done.5, bf16[1024,1024]{1,0:T(8,128)(2,1)S(1)} %order_rows.1.rows_ref, bf16[8,2,16,1024]{3,2,1,0:T(8,128)(2,1)S(1)} %collective-permute-done.7.last_ref, ...), custom_call_target="tpu_custom_call", output_to_operand_aliasing={{2}: (1, {})} | custom-call | flops 1207959552 | bytes 6291456 | tf_op jit(solution)/shard_map/final_update/pallas_call | solution.py:191
  (9 shorter events, 0.2 us)
Async XLA Ops:
  0.6 1.3 %copy-start = (bf16[2,512,512]{2,1,0:T(8,128)(2,1)S(1)}, bf16[2,512,512]{2,1,0:T(8,128)(2,1)}, u32[]{:S(2)}) copy-start(bf16[2,512,512]{2,1,0:T(8,128)(2,1)} %param.9) | copy-start | bytes 3145732
  0.6 31.9 %copy-start.6 = (s32[32]{0:T(128)S(1)}, s32[32]{0:T(128)}, u32[]{:S(2)}) copy-start(s32[32]{0:T(128)} %colmap_ref.1) | copy-start | bytes 388
  0.7 45.2 %copy-start.2 = (bf16[64,512]{1,0:T(8,128)(2,1)S(1)}, bf16[64,512]{1,0:T(8,128)(2,1)}, u32[]{:S(2)}) copy-start(bf16[64,512]{1,0:T(8,128)(2,1)} %sketch_ref.1) | copy-start | bytes 196612
  0.7 45.2 %copy-start.4 = (bf16[2,64,512]{2,1,0:T(8,128)(2,1)S(1)}, bf16[2,64,512]{2,1,0:T(8,128)(2,1)}, u32[]{:S(2)}) copy-start(bf16[2,64,512]{2,1,0:T(8,128)(2,1)} %right_ref.1) | copy-start | bytes 393220
  0.7 45.2 %copy-start.3 = (bf16[1,64,1024]{2,1,0:T(8,128)(2,1)S(1)}, bf16[1,64,1024]{2,1,0:T(8,128)(2,1)}, u32[]{:S(2)}) copy-start(bf16[1,64,1024]{2,1,0:T(8,128)(2,1)} %param.11) | copy-start | bytes 393220
  2.3 30.2 %collective-permute-start = (bf16[1,2,16,1024]{3,2,1,0:T(8,128)(2,1)S(1)}, bf16[1,2,16,1024]{3,2,1,0:T(8,128)(2,1)S(1)}, u32[]{:S(2)}, u32[]{:S(2)}) collective-permute-start(bf16[1,2,16,1024]{3,2,1,0:T(8,128)(2,1)S(1)} %convert_element_type.25), channel_id=1, source_target_pairs={{0,256},{16,272},{32,288},{48,304},{64,320},{80,336},{96,352},{112... | collective-permute-start | bytes 196616 | tf_op jit(solution)/shard_map/ppermute | solution.py:38
  33.8 16.5 %all-to-all-start.1 = ((bf16[16,2,8,128]{3,2,1,0:T(8,128)(2,1)}), bf16[16,2,8,128]{3,2,1,0:T(8,128)(2,1)S(1)}, u32[]{:S(2)}, u32[]{:S(2)}) async-start(bf16[16,2,8,128]{3,2,1,0:T(8,128)(2,1)} %bitcast.8), calls=%async_computation.1 | async-start | bytes 131072 | tf_op jit(solution)/shard_map/all_to_all | solution.py:253
  38.6 17.2 %collective-permute-start.1 = (bf16[2,2,16,1024]{3,2,1,0:T(8,128)(2,1)S(1)}, bf16[2,2,16,1024]{3,2,1,0:T(8,128)(2,1)S(1)}, u32[]{:S(2)}, u32[]{:S(2)}) collective-permute-start(bf16[2,2,16,1024]{3,2,1,0:T(8,128)(2,1)S(1)} %constant_dynamic-update-slice_fusion.refs_0_), channel_id=1, source_target_pairs={{0,128},{16,400},{32,160},{48,432},{64,192},{80,464},{96,224},{112... | collective-permute-start | bytes 393224 | tf_op jit(solution)/shard_map/ppermute | solution.py:38
  57.1 24.1 %all-to-all-start.2 = ((bf16[16,32,8,128]{3,2,1,0:T(8,128)(2,1)}), bf16[16,32,8,128]{3,2,1,0:T(8,128)(2,1)S(1)}, u32[]{:S(2)}, u32[]{:S(2)}) async-start(bf16[16,32,8,128]{3,2,1,0:T(8,128)(2,1)} %broadcast_in_dim.8), calls=%async_computation.2 | async-start | bytes 2097152 | tf_op jit(solution)/shard_map/all_to_all | solution.py:265
  60.7 15.3 %collective-permute-start.2 = (bf16[4,2,16,1024]{3,2,1,0:T(8,128)(2,1)S(1)}, bf16[4,2,16,1024]{3,2,1,0:T(8,128)(2,1)S(1)}, u32[]{:S(2)}, u32[]{:S(2)}) collective-permute-start(bf16[4,2,16,1024]{3,2,1,0:T(8,128)(2,1)S(1)} %stack_after.1.refs_0_), channel_id=1, source_target_pairs={{0,32},{16,48},{32,64},{48,80},{64,96},{80,112},{96,128},{112,144}... | collective-permute-start | bytes 786440 | tf_op jit(solution)/shard_map/ppermute | solution.py:38
  66.6 11.4 %collective-permute-start.4 = (bf16[4,2,16,1024]{3,2,1,0:T(8,128)(2,1)S(1)}, bf16[4,2,16,1024]{3,2,1,0:T(8,128)(2,1)S(1)}, u32[]{:S(2)}, u32[]{:S(2)}) collective-permute-start(bf16[4,2,16,1024]{3,2,1,0:T(8,128)(2,1)S(1)} %stack_after.1.refs_0_), channel_id=1, source_target_pairs={{0,64},{16,464},{32,96},{48,496},{64,128},{80,16},{96,160},{112,48... | collective-permute-start | bytes 786440 | tf_op jit(solution)/shard_map/ppermute | solution.py:38
  68.6 12.5 %collective-permute-start.3 = (bf16[4,2,16,1024]{3,2,1,0:T(8,128)(2,1)S(1)}, bf16[4,2,16,1024]{3,2,1,0:T(8,128)(2,1)S(1)}, u32[]{:S(2)}, u32[]{:S(2)}) collective-permute-start(bf16[4,2,16,1024]{3,2,1,0:T(8,128)(2,1)S(1)} %stack_after.1.refs_0_), channel_id=1, source_target_pairs={{0,480},{16,496},{32,0},{48,16},{64,32},{80,48},{96,64},{112,80},{... | collective-permute-start | bytes 786440 | tf_op jit(solution)/shard_map/ppermute | solution.py:38
  70.8 13.5 %collective-permute-start.5 = (bf16[4,2,16,1024]{3,2,1,0:T(8,128)(2,1)S(1)}, bf16[4,2,16,1024]{3,2,1,0:T(8,128)(2,1)}, u32[]{:S(2)}, u32[]{:S(2)}) collective-permute-start(bf16[4,2,16,1024]{3,2,1,0:T(8,128)(2,1)S(1)} %stack_after.1.refs_0_), channel_id=1, source_target_pairs={{0,16},{16,0},{32,48},{48,32},{64,80},{80,64},{96,112},{112,96},{1... | collective-permute-start | bytes 786440 | tf_op jit(solution)/shard_map/ppermute | solution.py:263
  76.0 8.3 %collective-permute-start.6 = (bf16[4,2,16,1024]{3,2,1,0:T(8,128)(2,1)S(1)}, bf16[4,2,16,1024]{3,2,1,0:T(8,128)(2,1)}, u32[]{:S(2)}, u32[]{:S(2)}) collective-permute-start(bf16[4,2,16,1024]{3,2,1,0:T(8,128)(2,1)S(1)} %collective-permute-done.2.refs_1_), channel_id=1, source_target_pairs={{0,16},{16,0},{32,48},{48,32},{64,80},{80,64},{96,112},{112,96},{1... | collective-permute-start | bytes 786440 | tf_op jit(solution)/shard_map/ppermute | solution.py:263
  81.2 4.7 %collective-permute-start.7 = (bf16[8,2,16,1024]{3,2,1,0:T(8,128)(2,1)S(1)}, bf16[8,2,16,1024]{3,2,1,0:T(8,128)(2,1)S(1)}, u32[]{:S(2)}, u32[]{:S(2)}) collective-permute-start(bf16[8,2,16,1024]{3,2,1,0:T(8,128)(2,1)S(1)} %hold.3.refs_2_), channel_id=1, source_target_pairs={{0,16},{16,0},{32,48},{48,32},{64,80},{80,64},{96,112},{112,96},{1... | collective-permute-start | bytes 1572872 | tf_op jit(solution)/shard_map/ppermute | solution.py:267
  85.5 1.2 %copy-start.1 = (bf16[1024,512]{1,0:T(8,128)(2,1)S(1)}, bf16[1024,512]{1,0:T(8,128)(2,1)}, u32[]{:S(2)}) copy-start(bf16[1024,512]{1,0:T(8,128)(2,1)} %tiles_ref.1) | copy-start | bytes 3145732
  85.5 1.2 %copy-start.5 = (s32[32,32]{1,0:T(8,128)S(1)}, s32[32,32]{1,0:T(8,128)}, u32[]{:S(2)}) copy-start(s32[32,32]{1,0:T(8,128)} %pattern_ref.1) | copy-start | bytes 12292

commit v5 on v4

--- a/solution.py
+++ b/solution.py
@@ -24,14 +24,6 @@
 
 def core_swap(z_count):
     return [(i, i ^ 1) for i in range(z_count * CORES)]
-
-
-def same_core(z_count):
-    return [[z * CORES + core for z in range(z_count)] for core in range(CORES)]
-
-
-def same_chip(z_count):
-    return [[z * CORES + core for core in range(CORES)] for z in range(z_count)]
 
 
 def shift(array, z_count, up, down):
@@ -227,9 +219,6 @@
     col_count = tile_size // piece
     z_count = col_count // CORES
     row_count = pattern.shape[0] // slots
-    col_index = lax.axis_index("col")
-    core = col_index % CORES
-
     lane_blocks = depth // LANES
     halves = piece // HALF
     parts = panel.reshape(slots, halves, HALF, lane_blocks, LANES).transpose(1, 3, 0, 2, 4)
@@ -249,12 +238,10 @@
     first_term = low_rank_term(left_factor[0], right_factor, sketch, parts)
     own = jnp.concatenate([own, half], axis=0)
     quarter = shift(own, z_count, z_count // 4, -(z_count // 4))
-    parts = parts.reshape(z_count, CORES, HALF, LANES)
-    parts = lax.all_to_all(parts, "col", 0, 0, axis_index_groups=same_core(z_count))
+    parts = parts.reshape(col_count, HALF, LANES)
+    parts = lax.all_to_all(parts, "col", 0, 0)
     own = stack_after([own, quarter], parts)
-    parts = lax.all_gather(parts, "col", axis=1, axis_index_groups=same_chip(z_count))
     parts = hold(parts, own, first_term)
-    parts = lax.dynamic_index_in_dim(parts, core, 2, keepdims=False)
     parts = parts.reshape(1, col_count, HALF, LANES)
     parts = jnp.broadcast_to(parts, (row_count, col_count, HALF, LANES))
 

time: 91.2 us -> 90.2 us (0.989)
  blocking collectives: 18.6 us -> 13.1 us
  waiting for transfers between devices: 7.1 us -> 10.4 us
  starting transfers between devices: 51.9 us -> 53.2 us
    ppermute x5, waiting for transfers between devices: 3.17 us -> 10.4 us  [shift(): return lax.ppermute(array, 'col', z_shift(z_count, up, down))]
    all_gather x1 -> x0, blocking collectives: 5.54 us -> none  [on_device(): lax.all_gather(parts, 'col', axis=1, axis_index_groups=same_chip(z_count))]
    all_to_all x1, waiting for transfers between devices: 3.93 us -> 0.01 us  [on_device(): parts = lax.all_to_all(parts, 'col', 0, 0)]
    all_to_all x1, starting transfers between devices: 4.85 us -> 7.54 us  [on_device(): parts = lax.all_to_all(parts, 'col', 0, 0)]
where the time goes in v5:
time: 90.2 us; the launch traced here: 89.6 us
  starting transfers between devices  53.2 us (59%)
  blocking collectives  13.1 us (15%)
  waiting for transfers between devices  10.4 us (12%)
  Pallas kernels  6.74 us (7%)
  local copies, waits for them, and re-layouts  4.46 us (5%)
  between operations  0.94 us (1%)
    ppermute x5, starting transfers between devices, shift(): return lax.ppermute(array, 'col', z_shift(z_count, up, down))  33.3 us
    all_to_all x1, blocking collectives, on_device(): parts = lax.all_to_all(parts, 'row', 0, 0)  13.1 us
    ppermute x5, waiting for transfers between devices, shift(): return lax.ppermute(array, 'col', z_shift(z_count, up, down))  10.4 us
    all_to_all x1, starting transfers between devices, on_device(): parts = lax.all_to_all(parts, 'col', 0, 0)  7.54 us
    ppermute x2, starting transfers between devices, on_device(): other = [lax.ppermute(part, 'col', core_swap(z_count)) for part in own]  6.24 us
    pallas_call x1, Pallas kernels, final_update(): pl.pallas_call(final_kernel, grid=(count // ROW_STEP,), out_shape=(jax.Sh...  3.83 us
    all_to_all x1, starting transfers between devices, on_device(): parts = lax.all_to_all(parts, 'row', 0, 0)  3.66 us
    ppermute x1, starting transfers between devices, on_device(): last = lax.ppermute(own[-1], 'col', core_swap(z_count))  2.5 us
  transfers between devices with their start and end apart: 10, of which 2 were waited for; matrix products, arithmetic and copies ran while one was open for 2% of the time, Pallas kernels for 2%

profile of v5, /device:TPU:1, one launch (start us, length us, event | category | flops | bytes accessed | tf_op | source)
XLA Modules:
  0.0 89.6 jit_solution(132091013243220149)
XLA Ops:
  0.6 0.0 copy-start
  0.6 0.0 copy-start.6
  0.7 0.0 copy-start.2
  0.7 0.0 copy-start.4
  0.7 0.0 copy-start.3
  0.7 0.9 %copy.19 = bf16[2,2,2,8,512]{4,3,1,0,2:T(8,128)(2,1)S(1)} copy(bf16[2,2,2,8,512]{4,3,2,1,0:T(8,128)(2,1)} %bitcast.34) | data formatting | bytes 131072 | tf_op jit(solution)/shard_map/reshape | solution.py:231
  1.6 0.3 copy-done
  1.9 0.3 fusion.1
  2.2 0.1 copy.14
  2.3 16.3 %collective-permute-start = (bf16[1,2,16,1024]{3,2,1,0:T(8,128)(2,1)S(1)}, bf16[1,2,16,1024]{3,2,1,0:T(8,128)(2,1)S(1)}, u32[]{:S(2)}, u32[]{:S(2)}) collective-permute-start(bf16[1,2,16,1024]{3,2,1,0:T(8,128)(2,1)S(1)} %convert_element_type.25), channel_id=1, source_target_pairs={{0,256},{16,272},{32,288},{48,304},{64,320},{80,336},{96,352},{112... | collective-permute-start | bytes 196616 | tf_op jit(solution)/shard_map/ppermute | solution.py:30
  18.6 0.9 copy.15
  19.5 13.1 %all_to_all.15 = bf16[16,2,8,128]{3,2,1,0:T(8,128)(2,1)S(1)} all-to-all(bf16[16,2,8,128]{3,2,1,0:T(8,128)(2,1)S(1)} %bitcast.36), channel_id=1, replica_groups=mesh['col'=32,'row'=16] {'row'}, dimensions={0} | all-to-all | bytes 131072 | tf_op jit(solution)/shard_map/all_to_all | solution.py:226
  32.6 0.0 collective-permute-done._
  32.6 0.0 copy-done.6
  32.6 1.2 %select_tiles.1._ = bf16[32,8,128]{2,1,0:T(8,128)(2,1)} custom-call(s32[32]{0:T(128)S(1)} %copy-done.6, bf16[32,8,128]{2,1,0:T(8,128)(2,1)S(1)} %bitcast.28, bf16[1,2,16,1024]{3,2,1,0:T(8,128)(2,1)S(1)} %collective-permute-done._), custom_call_target="tpu_custom_call" | custom-call | tf_op jit(solution)/shard_map/select_tiles/pallas_call | solution.py:103
  33.8 7.5 %all-to-all-start.1 = ((bf16[32,8,128]{2,1,0:T(8,128)(2,1)}), bf16[32,8,128]{2,1,0:T(8,128)(2,1)S(1)}, u32[]{:S(2)}, u32[]{:S(2)}) async-start(bf16[32,8,128]{2,1,0:T(8,128)(2,1)} %select_tiles.1._), calls=%async_computation.1 | async-start | bytes 131072 | tf_op jit(solution)/shard_map/all_to_all | solution.py:242
  41.3 7.2 %collective-permute-start.1 = (bf16[2,2,16,1024]{3,2,1,0:T(8,128)(2,1)S(1)}, bf16[2,2,16,1024]{3,2,1,0:T(8,128)(2,1)S(1)}, u32[]{:S(2)}, u32[]{:S(2)}) collective-permute-start(bf16[2,2,16,1024]{3,2,1,0:T(8,128)(2,1)S(1)} %constant_dynamic-update-slice_fusion.refs_0_), channel_id=1, source_target_pairs={{0,128},{16,400},{32,160},{48,432},{64,192},{80,464},{96,224},{112... | collective-permute-start | bytes 393224 | tf_op jit(solution)/shard_map/ppermute | solution.py:30
  48.6 0.0 copy-done.2
  48.6 0.0 copy-done.4
  48.6 0.0 copy-done.3
  48.6 0.5 low_rank_term.1.refs_1_.first_ref
  49.1 6.9 %collective-permute-done.1.refs_1_ = bf16[2,2,16,1024]{3,2,1,0:T(8,128)(2,1)S(1)} collective-permute-done((bf16[2,2,16,1024]{3,2,1,0:T(8,128)(2,1)S(1)}, bf16[2,2,16,1024]{3,2,1,0:T(8,128)(2,1)S(1)}, u32[]{:S(2)}, u32[]{:S(2)}) %collective-permute-start.1) | collective-permute-done | bytes 131104 | tf_op jit(solution)/shard_map/ppermute | solution.py:30
  56.0 0.0 all-to-all-done.1.refs_2_.array_ref
  56.0 1.2 %broadcast_in_dim.2 = bf16[16,32,8,128]{3,2,1,0:T(8,128)(2,1)} broadcast(bf16[32,8,128]{2,1,0:T(8,128)(2,1)S(1)} %hold.2), dimensions={1,2,3} | broadcast | bytes 1114112 | tf_op jit(solution)/shard_map/broadcast_in_dim | solution.py:246
  57.2 3.7 %all-to-all-start.2 = ((bf16[16,32,8,128]{3,2,1,0:T(8,128)(2,1)}), bf16[16,32,8,128]{3,2,1,0:T(8,128)(2,1)S(1)}, u32[]{:S(2)}, u32[]{:S(2)}) async-start(bf16[16,32,8,128]{3,2,1,0:T(8,128)(2,1)} %broadcast_in_dim.2), calls=%async_computation.2 | async-start | bytes 2097152 | tf_op jit(solution)/shard_map/all_to_all | solution.py:252
  60.9 2.2 %collective-permute-start.2 = (bf16[4,2,16,1024]{3,2,1,0:T(8,128)(2,1)S(1)}, bf16[4,2,16,1024]{3,2,1,0:T(8,128)(2,1)S(1)}, u32[]{:S(2)}, u32[]{:S(2)}) collective-permute-start(bf16[4,2,16,1024]{3,2,1,0:T(8,128)(2,1)S(1)} %stack_after.1.refs_0_), channel_id=1, source_target_pairs={{0,32},{16,48},{32,64},{48,80},{64,96},{80,112},{96,128},{112,144}... | collective-permute-start | bytes 786440 | tf_op jit(solution)/shard_map/ppermute | solution.py:30
  63.1 5.6 %collective-permute-start.4 = (bf16[4,2,16,1024]{3,2,1,0:T(8,128)(2,1)S(1)}, bf16[4,2,16,1024]{3,2,1,0:T(8,128)(2,1)S(1)}, u32[]{:S(2)}, u32[]{:S(2)}) collective-permute-start(bf16[4,2,16,1024]{3,2,1,0:T(8,128)(2,1)S(1)} %stack_after.1.refs_0_), channel_id=1, source_target_pairs={{0,64},{16,464},{32,96},{48,496},{64,128},{80,16},{96,160},{112,48... | collective-permute-start | bytes 786440 | tf_op jit(solution)/shard_map/ppermute | solution.py:30
  68.7 1.9 %collective-permute-start.3 = (bf16[4,2,16,1024]{3,2,1,0:T(8,128)(2,1)S(1)}, bf16[4,2,16,1024]{3,2,1,0:T(8,128)(2,1)S(1)}, u32[]{:S(2)}, u32[]{:S(2)}) collective-permute-start(bf16[4,2,16,1024]{3,2,1,0:T(8,128)(2,1)S(1)} %stack_after.1.refs_0_), channel_id=1, source_target_pairs={{0,480},{16,496},{32,0},{48,16},{64,32},{80,48},{96,64},{112,80},{... | collective-permute-start | bytes 786440 | tf_op jit(solution)/shard_map/ppermute | solution.py:30
  70.7 4.3 %collective-permute-start.5 = (bf16[4,2,16,1024]{3,2,1,0:T(8,128)(2,1)S(1)}, bf16[4,2,16,1024]{3,2,1,0:T(8,128)(2,1)}, u32[]{:S(2)}, u32[]{:S(2)}) collective-permute-start(bf16[4,2,16,1024]{3,2,1,0:T(8,128)(2,1)S(1)} %stack_after.1.refs_0_), channel_id=1, source_target_pairs={{0,16},{16,0},{32,48},{48,32},{64,80},{80,64},{96,112},{112,96},{1... | collective-permute-start | bytes 786440 | tf_op jit(solution)/shard_map/ppermute | solution.py:250
  75.0 0.0 collective-permute-done.2.refs_1_
  75.0 1.9 %collective-permute-start.6 = (bf16[4,2,16,1024]{3,2,1,0:T(8,128)(2,1)S(1)}, bf16[4,2,16,1024]{3,2,1,0:T(8,128)(2,1)}, u32[]{:S(2)}, u32[]{:S(2)}) collective-permute-start(bf16[4,2,16,1024]{3,2,1,0:T(8,128)(2,1)S(1)} %collective-permute-done.2.refs_1_), channel_id=1, source_target_pairs={{0,16},{16,0},{32,48},{48,32},{64,80},{80,64},{96,112},{112,96},{1... | collective-permute-start | bytes 786440 | tf_op jit(solution)/shard_map/ppermute | solution.py:250
  76.9 0.0 collective-permute-done.4
  77.0 3.5 %collective-permute-done.3 = bf16[4,2,16,1024]{3,2,1,0:T(8,128)(2,1)S(1)} collective-permute-done((bf16[4,2,16,1024]{3,2,1,0:T(8,128)(2,1)S(1)}, bf16[4,2,16,1024]{3,2,1,0:T(8,128)(2,1)S(1)}, u32[]{:S(2)}, u32[]{:S(2)}) %collective-permute-start.3) | collective-permute-done | bytes 262176 | tf_op jit(solution)/shard_map/ppermute | solution.py:30
  80.5 0.0 all-to-all-done.2.refs_0_
  80.5 0.1 hold.3.refs_2_
  80.6 2.5 %collective-permute-start.7 = (bf16[8,2,16,1024]{3,2,1,0:T(8,128)(2,1)S(1)}, bf16[8,2,16,1024]{3,2,1,0:T(8,128)(2,1)S(1)}, u32[]{:S(2)}, u32[]{:S(2)}) collective-permute-start(bf16[8,2,16,1024]{3,2,1,0:T(8,128)(2,1)S(1)} %hold.3.refs_2_), channel_id=1, source_target_pairs={{0,16},{16,0},{32,48},{48,32},{64,80},{80,64},{96,112},{112,96},{1... | collective-permute-start | bytes 1572872 | tf_op jit(solution)/shard_map/ppermute | solution.py:254
  83.1 0.3 copy.16
  83.4 0.0 collective-permute-done.5.refs_3_
  83.4 0.0 collective-permute-done.6.refs_4_
  83.4 1.2 %order_rows.1.rows_ref = bf16[1024,1024]{1,0:T(8,128)(2,1)S(1)} custom-call(bf16[4,2,16,1024]{3,2,1,0:T(8,128)(2,1)S(1)} %stack_after.1.refs_0_, bf16[4,2,16,1024]{3,2,1,0:T(8,128)(2,1)S(1)} %collective-permute-done.2.refs_1_, bf16[8,2,16,1024]{3,2,1,0:T(8,128)(2,1)S(1)} %hold.3.refs_2_, bf16[4,2,16,1024]{3,2,1,0:T(8,128)(2,1)} %collective-permute-done.5.refs_3_, ...), custom_call_target="tpu_custom_call" | custom-call | tf_op jit(solution)/shard_map/order_rows/pallas_call | solution.py:144
  84.6 0.0 copy-start.1
  84.6 0.0 copy-start.5
  84.6 0.3 fusion
  84.9 0.1 pad_maximum_fusion.right_ref
  85.0 0.0 collective-permute-done.7.last_ref
  85.0 0.8 copy-done.1
  85.8 0.0 copy-done.5
  85.8 3.8 %final_update.1 = (bf16[1024,512]{1,0:T(8,128)(2,1)}, bf16[64,1024]{1,0:T(8,128)(2,1)}, bf16[1024,1024]{1,0:T(8,128)(2,1)S(1)}) custom-call(s32[32,32]{1,0:T(8,128)S(1)} %copy-done.5, bf16[1024,1024]{1,0:T(8,128)(2,1)S(1)} %order_rows.1.rows_ref, bf16[8,2,16,1024]{3,2,1,0:T(8,128)(2,1)S(1)} %collective-permute-done.7.last_ref, ...), custom_call_target="tpu_custom_call", output_to_operand_aliasing={{2}: (1, {})} | custom-call | flops 1207959552 | bytes 6291456 | tf_op jit(solution)/shard_map/final_update/pallas_call | solution.py:183
  (7 shorter events, 0.2 us)
Async XLA Ops:
  0.6 1.3 %copy-start = (bf16[2,512,512]{2,1,0:T(8,128)(2,1)S(1)}, bf16[2,512,512]{2,1,0:T(8,128)(2,1)}, u32[]{:S(2)}) copy-start(bf16[2,512,512]{2,1,0:T(8,128)(2,1)} %param.9) | copy-start | bytes 3145732
  0.6 31.9 %copy-start.6 = (s32[32]{0:T(128)S(1)}, s32[32]{0:T(128)}, u32[]{:S(2)}) copy-start(s32[32]{0:T(128)} %colmap_ref.1) | copy-start | bytes 388
  0.7 47.9 %copy-start.2 = (bf16[64,512]{1,0:T(8,128)(2,1)S(1)}, bf16[64,512]{1,0:T(8,128)(2,1)}, u32[]{:S(2)}) copy-start(bf16[64,512]{1,0:T(8,128)(2,1)} %sketch_ref.1) | copy-start | bytes 196612
  0.7 47.9 %copy-start.4 = (bf16[2,64,512]{2,1,0:T(8,128)(2,1)S(1)}, bf16[2,64,512]{2,1,0:T(8,128)(2,1)}, u32[]{:S(2)}) copy-start(bf16[2,64,512]{2,1,0:T(8,128)(2,1)} %right_ref.1) | copy-start | bytes 393220
  0.7 47.9 %copy-start.3 = (bf16[1,64,1024]{2,1,0:T(8,128)(2,1)S(1)}, bf16[1,64,1024]{2,1,0:T(8,128)(2,1)}, u32[]{:S(2)}) copy-start(bf16[1,64,1024]{2,1,0:T(8,128)(2,1)} %param.11) | copy-start | bytes 393220
  2.3 30.2 %collective-permute-start = (bf16[1,2,16,1024]{3,2,1,0:T(8,128)(2,1)S(1)}, bf16[1,2,16,1024]{3,2,1,0:T(8,128)(2,1)S(1)}, u32[]{:S(2)}, u32[]{:S(2)}) collective-permute-start(bf16[1,2,16,1024]{3,2,1,0:T(8,128)(2,1)S(1)} %convert_element_type.25), channel_id=1, source_target_pairs={{0,256},{16,272},{32,288},{48,304},{64,320},{80,336},{96,352},{112... | collective-permute-start | bytes 196616 | tf_op jit(solution)/shard_map/ppermute | solution.py:30
  33.8 22.2 %all-to-all-start.1 = ((bf16[32,8,128]{2,1,0:T(8,128)(2,1)}), bf16[32,8,128]{2,1,0:T(8,128)(2,1)S(1)}, u32[]{:S(2)}, u32[]{:S(2)}) async-start(bf16[32,8,128]{2,1,0:T(8,128)(2,1)} %select_tiles.1._), calls=%async_computation.1 | async-start | bytes 131072 | tf_op jit(solution)/shard_map/all_to_all | solution.py:242
  41.3 14.7 %collective-permute-start.1 = (bf16[2,2,16,1024]{3,2,1,0:T(8,128)(2,1)S(1)}, bf16[2,2,16,1024]{3,2,1,0:T(8,128)(2,1)S(1)}, u32[]{:S(2)}, u32[]{:S(2)}) collective-permute-start(bf16[2,2,16,1024]{3,2,1,0:T(8,128)(2,1)S(1)} %constant_dynamic-update-slice_fusion.refs_0_), channel_id=1, source_target_pairs={{0,128},{16,400},{32,160},{48,432},{64,192},{80,464},{96,224},{112... | collective-permute-start | bytes 393224 | tf_op jit(solution)/shard_map/ppermute | solution.py:30
  57.2 23.3 %all-to-all-start.2 = ((bf16[16,32,8,128]{3,2,1,0:T(8,128)(2,1)}), bf16[16,32,8,128]{3,2,1,0:T(8,128)(2,1)S(1)}, u32[]{:S(2)}, u32[]{:S(2)}) async-start(bf16[16,32,8,128]{3,2,1,0:T(8,128)(2,1)} %broadcast_in_dim.2), calls=%async_computation.2 | async-start | bytes 2097152 | tf_op jit(solution)/shard_map/all_to_all | solution.py:252
  60.9 14.1 %collective-permute-start.2 = (bf16[4,2,16,1024]{3,2,1,0:T(8,128)(2,1)S(1)}, bf16[4,2,16,1024]{3,2,1,0:T(8,128)(2,1)S(1)}, u32[]{:S(2)}, u32[]{:S(2)}) collective-permute-start(bf16[4,2,16,1024]{3,2,1,0:T(8,128)(2,1)S(1)} %stack_after.1.refs_0_), channel_id=1, source_target_pairs={{0,32},{16,48},{32,64},{48,80},{64,96},{80,112},{96,128},{112,144}... | collective-permute-start | bytes 786440 | tf_op jit(solution)/shard_map/ppermute | solution.py:30
  63.1 13.8 %collective-permute-start.4 = (bf16[4,2,16,1024]{3,2,1,0:T(8,128)(2,1)S(1)}, bf16[4,2,16,1024]{3,2,1,0:T(8,128)(2,1)S(1)}, u32[]{:S(2)}, u32[]{:S(2)}) collective-permute-start(bf16[4,2,16,1024]{3,2,1,0:T(8,128)(2,1)S(1)} %stack_after.1.refs_0_), channel_id=1, source_target_pairs={{0,64},{16,464},{32,96},{48,496},{64,128},{80,16},{96,160},{112,48... | collective-permute-start | bytes 786440 | tf_op jit(solution)/shard_map/ppermute | solution.py:30
  68.7 11.7 %collective-permute-start.3 = (bf16[4,2,16,1024]{3,2,1,0:T(8,128)(2,1)S(1)}, bf16[4,2,16,1024]{3,2,1,0:T(8,128)(2,1)S(1)}, u32[]{:S(2)}, u32[]{:S(2)}) collective-permute-start(bf16[4,2,16,1024]{3,2,1,0:T(8,128)(2,1)S(1)} %stack_after.1.refs_0_), channel_id=1, source_target_pairs={{0,480},{16,496},{32,0},{48,16},{64,32},{80,48},{96,64},{112,80},{... | collective-permute-start | bytes 786440 | tf_op jit(solution)/shard_map/ppermute | solution.py:30
  70.7 12.7 %collective-permute-start.5 = (bf16[4,2,16,1024]{3,2,1,0:T(8,128)(2,1)S(1)}, bf16[4,2,16,1024]{3,2,1,0:T(8,128)(2,1)}, u32[]{:S(2)}, u32[]{:S(2)}) collective-permute-start(bf16[4,2,16,1024]{3,2,1,0:T(8,128)(2,1)S(1)} %stack_after.1.refs_0_), channel_id=1, source_target_pairs={{0,16},{16,0},{32,48},{48,32},{64,80},{80,64},{96,112},{112,96},{1... | collective-permute-start | bytes 786440 | tf_op jit(solution)/shard_map/ppermute | solution.py:250
  75.0 8.4 %collective-permute-start.6 = (bf16[4,2,16,1024]{3,2,1,0:T(8,128)(2,1)S(1)}, bf16[4,2,16,1024]{3,2,1,0:T(8,128)(2,1)}, u32[]{:S(2)}, u32[]{:S(2)}) collective-permute-start(bf16[4,2,16,1024]{3,2,1,0:T(8,128)(2,1)S(1)} %collective-permute-done.2.refs_1_), channel_id=1, source_target_pairs={{0,16},{16,0},{32,48},{48,32},{64,80},{80,64},{96,112},{112,96},{1... | collective-permute-start | bytes 786440 | tf_op jit(solution)/shard_map/ppermute | solution.py:250
  80.6 4.4 %collective-permute-start.7 = (bf16[8,2,16,1024]{3,2,1,0:T(8,128)(2,1)S(1)}, bf16[8,2,16,1024]{3,2,1,0:T(8,128)(2,1)S(1)}, u32[]{:S(2)}, u32[]{:S(2)}) collective-permute-start(bf16[8,2,16,1024]{3,2,1,0:T(8,128)(2,1)S(1)} %hold.3.refs_2_), channel_id=1, source_target_pairs={{0,16},{16,0},{32,48},{48,32},{64,80},{80,64},{96,112},{112,96},{1... | collective-permute-start | bytes 1572872 | tf_op jit(solution)/shard_map/ppermute | solution.py:254
  84.6 1.2 %copy-start.1 = (bf16[1024,512]{1,0:T(8,128)(2,1)S(1)}, bf16[1024,512]{1,0:T(8,128)(2,1)}, u32[]{:S(2)}) copy-start(bf16[1024,512]{1,0:T(8,128)(2,1)} %tiles_ref.1) | copy-start | bytes 3145732
  84.6 1.2 %copy-start.5 = (s32[32,32]{1,0:T(8,128)S(1)}, s32[32,32]{1,0:T(8,128)}, u32[]{:S(2)}) copy-start(s32[32,32]{1,0:T(8,128)} %pattern_ref.1) | copy-start | bytes 12292

commit v6 on v5

--- a/solution.py
+++ b/solution.py
@@ -71,6 +71,24 @@
         compiler_params=pltpu.CompilerParams(vmem_limit_bytes=4 * 1024 * 1024),
         name="hold",
     )(array, *earlier)
+
+
+def spread_kernel(parts_ref, *refs):
+    out_ref = refs[-1]
+    part = parts_ref[...]
+    for row in range(out_ref.shape[0]):
+        out_ref[row] = part
+
+
+def spread(parts, row_count, *earlier):
+    return pl.pallas_call(
+        spread_kernel,
+        out_shape=jax.ShapeDtypeStruct((row_count,) + parts.shape, parts.dtype),
+        in_specs=[VMEM] * (1 + len(earlier)),
+        out_specs=VMEM,
+        compiler_params=pltpu.CompilerParams(vmem_limit_bytes=4 * 1024 * 1024),
+        name="spread",
+    )(parts, *earlier)
 
 
 def low_rank_kernel(left_ref, right_ref, sketch_ref, _, out_ref):
@@ -241,9 +259,7 @@
     parts = parts.reshape(col_count, HALF, LANES)
     parts = lax.all_to_all(parts, "col", 0, 0)
     own = stack_after([own, quarter], parts)
-    parts = hold(parts, own, first_term)
-    parts = parts.reshape(1, col_count, HALF, LANES)
-    parts = jnp.broadcast_to(parts, (row_count, col_count, HALF, LANES))
+    parts = spread(parts, row_count, own, first_term)
 
     near = [shift(own, z_count, up, down) for up, down in ((1, 1), (-1, -1), (2, -2))]
     own = [own, near[0]]

time: 90.2 us -> 90.2 us (level)
  local copies, waits for them, and re-layouts: 4.46 us -> 3.28 us
  Pallas kernels: 6.74 us -> 7.9 us
    pallas_call x0 -> x1, Pallas kernels: none -> 1.18 us  [spread(): pl.pallas_call(spread_kernel, out_shape=jax.ShapeDtypeStruct((row_count,)...]
    broadcast_in_dim x1 -> x0, local copies, waits for them, and re-layouts: 1.17 us -> none  [on_device(): parts = jnp.broadcast_to(parts, (row_count, col_count, HALF, LANES))]
where the time goes in v6:
time: 90.2 us; the launch traced here: 89.6 us
  starting transfers between devices  53.2 us (59%)
  blocking collectives  13.1 us (15%)
  waiting for transfers between devices  10.4 us (12%)
  Pallas kernels  7.9 us (9%)
  local copies, waits for them, and re-layouts  3.28 us (4%)
  between operations  0.93 us (1%)
    ppermute x5, starting transfers between devices, shift(): return lax.ppermute(array, 'col', z_shift(z_count, up, down))  33.3 us
    all_to_all x1, blocking collectives, on_device(): parts = lax.all_to_all(parts, 'row', 0, 0)  13.1 us
    ppermute x5, waiting for transfers between devices, shift(): return lax.ppermute(array, 'col', z_shift(z_count, up, down))  10.4 us
    all_to_all x1, starting transfers between devices, on_device(): parts = lax.all_to_all(parts, 'col', 0, 0)  7.53 us
    ppermute x2, starting transfers between devices, on_device(): other = [lax.ppermute(part, 'col', core_swap(z_count)) for part in own]  6.24 us
    pallas_call x1, Pallas kernels, final_update(): pl.pallas_call(final_kernel, grid=(count // ROW_STEP,), out_shape=(jax.Sh...  3.83 us
    all_to_all x1, starting transfers between devices, on_device(): parts = lax.all_to_all(parts, 'row', 0, 0)  3.66 us
    ppermute x1, starting transfers between devices, on_device(): last = lax.ppermute(own[-1], 'col', core_swap(z_count))  2.5 us
  transfers between devices with their start and end apart: 10, of which 2 were waited for; matrix products, arithmetic and copies ran while one was open for 2% of the time, Pallas kernels for 2%

profile of v6, /device:TPU:1, one launch (start us, length us, event | category | flops | bytes accessed | tf_op | source)
XLA Modules:
  0.0 89.6 jit_solution(2004308579985100112)
XLA Ops:
  0.6 0.0 copy-start
  0.6 0.0 copy-start.6
  0.7 0.0 copy-start.2
  0.7 0.0 copy-start.4
  0.7 0.0 copy-start.3
  0.7 0.9 %copy.18 = bf16[2,2,2,8,512]{4,3,1,0,2:T(8,128)(2,1)S(1)} copy(bf16[2,2,2,8,512]{4,3,2,1,0:T(8,128)(2,1)} %bitcast.34) | data formatting | bytes 131072 | tf_op jit(solution)/shard_map/reshape | solution.py:249
  1.6 0.3 copy-done
  1.9 0.3 fusion.1
  2.2 0.1 copy.13
  2.3 16.3 %collective-permute-start = (bf16[1,2,16,1024]{3,2,1,0:T(8,128)(2,1)S(1)}, bf16[1,2,16,1024]{3,2,1,0:T(8,128)(2,1)S(1)}, u32[]{:S(2)}, u32[]{:S(2)}) collective-permute-start(bf16[1,2,16,1024]{3,2,1,0:T(8,128)(2,1)S(1)} %convert_element_type.25), channel_id=1, source_target_pairs={{0,256},{16,272},{32,288},{48,304},{64,320},{80,336},{96,352},{112... | collective-permute-start | bytes 196616 | tf_op jit(solution)/shard_map/ppermute | solution.py:30
  18.6 0.9 copy.14
  19.5 13.1 %all_to_all.15 = bf16[16,2,8,128]{3,2,1,0:T(8,128)(2,1)S(1)} all-to-all(bf16[16,2,8,128]{3,2,1,0:T(8,128)(2,1)S(1)} %bitcast.36), channel_id=1, replica_groups=mesh['col'=32,'row'=16] {'row'}, dimensions={0} | all-to-all | bytes 131072 | tf_op jit(solution)/shard_map/all_to_all | solution.py:244
  32.6 0.0 collective-permute-done._
  32.6 0.0 copy-done.6
  32.6 1.2 %select_tiles.1._ = bf16[32,8,128]{2,1,0:T(8,128)(2,1)} custom-call(s32[32]{0:T(128)S(1)} %copy-done.6, bf16[32,8,128]{2,1,0:T(8,128)(2,1)S(1)} %bitcast.28, bf16[1,2,16,1024]{3,2,1,0:T(8,128)(2,1)S(1)} %collective-permute-done._), custom_call_target="tpu_custom_call" | custom-call | tf_op jit(solution)/shard_map/select_tiles/pallas_call | solution.py:121
  33.8 7.5 %all-to-all-start.1 = ((bf16[32,8,128]{2,1,0:T(8,128)(2,1)}), bf16[32,8,128]{2,1,0:T(8,128)(2,1)S(1)}, u32[]{:S(2)}, u32[]{:S(2)}) async-start(bf16[32,8,128]{2,1,0:T(8,128)(2,1)} %select_tiles.1._), calls=%async_computation.1 | async-start | bytes 131072 | tf_op jit(solution)/shard_map/all_to_all | solution.py:260
  41.3 7.2 %collective-permute-start.1 = (bf16[2,2,16,1024]{3,2,1,0:T(8,128)(2,1)S(1)}, bf16[2,2,16,1024]{3,2,1,0:T(8,128)(2,1)S(1)}, u32[]{:S(2)}, u32[]{:S(2)}) collective-permute-start(bf16[2,2,16,1024]{3,2,1,0:T(8,128)(2,1)S(1)} %constant_dynamic-update-slice_fusion.refs_0_), channel_id=1, source_target_pairs={{0,128},{16,400},{32,160},{48,432},{64,192},{80,464},{96,224},{112... | collective-permute-start | bytes 393224 | tf_op jit(solution)/shard_map/ppermute | solution.py:30
  48.6 0.0 copy-done.2
  48.6 0.0 copy-done.4
  48.6 0.0 copy-done.3
  48.6 0.5 low_rank_term.1.refs_1_.first_ref
  49.1 6.9 %collective-permute-done.1.refs_1_ = bf16[2,2,16,1024]{3,2,1,0:T(8,128)(2,1)S(1)} collective-permute-done((bf16[2,2,16,1024]{3,2,1,0:T(8,128)(2,1)S(1)}, bf16[2,2,16,1024]{3,2,1,0:T(8,128)(2,1)S(1)}, u32[]{:S(2)}, u32[]{:S(2)}) %collective-permute-start.1) | collective-permute-done | bytes 131104 | tf_op jit(solution)/shard_map/ppermute | solution.py:30
  56.0 0.0 all-to-all-done.1.refs_2_.parts_ref
  56.0 1.2 %spread.1 = bf16[16,32,8,128]{3,2,1,0:T(8,128)(2,1)} custom-call(bf16[32,8,128]{2,1,0:T(8,128)(2,1)S(1)} %all-to-all-done.1.refs_2_.parts_ref, bf16[4,2,16,1024]{3,2,1,0:T(8,128)(2,1)S(1)} %stack_after.1.refs_0_, f32[64,1024]{1,0:T(8,128)S(1)} %low_rank_term.1.refs_1_.first_ref), custom_call_target="tpu_custom_call" | custom-call | tf_op jit(solution)/shard_map/spread/pallas_call | solution.py:84
  57.2 3.7 %all-to-all-start.2 = ((bf16[16,32,8,128]{3,2,1,0:T(8,128)(2,1)}), bf16[16,32,8,128]{3,2,1,0:T(8,128)(2,1)S(1)}, u32[]{:S(2)}, u32[]{:S(2)}) async-start(bf16[16,32,8,128]{3,2,1,0:T(8,128)(2,1)} %spread.1), calls=%async_computation.2 | async-start | bytes 2097152 | tf_op jit(solution)/shard_map/all_to_all | solution.py:268
  60.8 2.2 %collective-permute-start.2 = (bf16[4,2,16,1024]{3,2,1,0:T(8,128)(2,1)S(1)}, bf16[4,2,16,1024]{3,2,1,0:T(8,128)(2,1)S(1)}, u32[]{:S(2)}, u32[]{:S(2)}) collective-permute-start(bf16[4,2,16,1024]{3,2,1,0:T(8,128)(2,1)S(1)} %stack_after.1.refs_0_), channel_id=1, source_target_pairs={{0,32},{16,48},{32,64},{48,80},{64,96},{80,112},{96,128},{112,144}... | collective-permute-start | bytes 786440 | tf_op jit(solution)/shard_map/ppermute | solution.py:30
  63.1 5.6 %collective-permute-start.4 = (bf16[4,2,16,1024]{3,2,1,0:T(8,128)(2,1)S(1)}, bf16[4,2,16,1024]{3,2,1,0:T(8,128)(2,1)S(1)}, u32[]{:S(2)}, u32[]{:S(2)}) collective-permute-start(bf16[4,2,16,1024]{3,2,1,0:T(8,128)(2,1)S(1)} %stack_after.1.refs_0_), channel_id=1, source_target_pairs={{0,64},{16,464},{32,96},{48,496},{64,128},{80,16},{96,160},{112,48... | collective-permute-start | bytes 786440 | tf_op jit(solution)/shard_map/ppermute | solution.py:30
  68.7 1.9 %collective-permute-start.3 = (bf16[4,2,16,1024]{3,2,1,0:T(8,128)(2,1)S(1)}, bf16[4,2,16,1024]{3,2,1,0:T(8,128)(2,1)S(1)}, u32[]{:S(2)}, u32[]{:S(2)}) collective-permute-start(bf16[4,2,16,1024]{3,2,1,0:T(8,128)(2,1)S(1)} %stack_after.1.refs_0_), channel_id=1, source_target_pairs={{0,480},{16,496},{32,0},{48,16},{64,32},{80,48},{96,64},{112,80},{... | collective-permute-start | bytes 786440 | tf_op jit(solution)/shard_map/ppermute | solution.py:30
  70.6 4.3 %collective-permute-start.5 = (bf16[4,2,16,1024]{3,2,1,0:T(8,128)(2,1)S(1)}, bf16[4,2,16,1024]{3,2,1,0:T(8,128)(2,1)}, u32[]{:S(2)}, u32[]{:S(2)}) collective-permute-start(bf16[4,2,16,1024]{3,2,1,0:T(8,128)(2,1)S(1)} %stack_after.1.refs_0_), channel_id=1, source_target_pairs={{0,16},{16,0},{32,48},{48,32},{64,80},{80,64},{96,112},{112,96},{1... | collective-permute-start | bytes 786440 | tf_op jit(solution)/shard_map/ppermute | solution.py:266
  75.0 0.0 collective-permute-done.2.refs_1_
  75.0 1.9 %collective-permute-start.6 = (bf16[4,2,16,1024]{3,2,1,0:T(8,128)(2,1)S(1)}, bf16[4,2,16,1024]{3,2,1,0:T(8,128)(2,1)}, u32[]{:S(2)}, u32[]{:S(2)}) collective-permute-start(bf16[4,2,16,1024]{3,2,1,0:T(8,128)(2,1)S(1)} %collective-permute-done.2.refs_1_), channel_id=1, source_target_pairs={{0,16},{16,0},{32,48},{48,32},{64,80},{80,64},{96,112},{112,96},{1... | collective-permute-start | bytes 786440 | tf_op jit(solution)/shard_map/ppermute | solution.py:266
  76.9 0.0 collective-permute-done.4
  76.9 3.5 %collective-permute-done.3 = bf16[4,2,16,1024]{3,2,1,0:T(8,128)(2,1)S(1)} collective-permute-done((bf16[4,2,16,1024]{3,2,1,0:T(8,128)(2,1)S(1)}, bf16[4,2,16,1024]{3,2,1,0:T(8,128)(2,1)S(1)}, u32[]{:S(2)}, u32[]{:S(2)}) %collective-permute-start.3) | collective-permute-done | bytes 262176 | tf_op jit(solution)/shard_map/ppermute | solution.py:30
  80.5 0.0 all-to-all-done.2.refs_0_
  80.5 0.1 hold.1.refs_2_
  80.6 2.5 %collective-permute-start.7 = (bf16[8,2,16,1024]{3,2,1,0:T(8,128)(2,1)S(1)}, bf16[8,2,16,1024]{3,2,1,0:T(8,128)(2,1)S(1)}, u32[]{:S(2)}, u32[]{:S(2)}) collective-permute-start(bf16[8,2,16,1024]{3,2,1,0:T(8,128)(2,1)S(1)} %hold.1.refs_2_), channel_id=1, source_target_pairs={{0,16},{16,0},{32,48},{48,32},{64,80},{80,64},{96,112},{112,96},{1... | collective-permute-start | bytes 1572872 | tf_op jit(solution)/shard_map/ppermute | solution.py:270
  83.1 0.3 copy.15
  83.4 0.0 collective-permute-done.5.refs_3_
  83.4 0.0 collective-permute-done.6.refs_4_
  83.4 1.2 %order_rows.1.rows_ref = bf16[1024,1024]{1,0:T(8,128)(2,1)S(1)} custom-call(bf16[4,2,16,1024]{3,2,1,0:T(8,128)(2,1)S(1)} %stack_after.1.refs_0_, bf16[4,2,16,1024]{3,2,1,0:T(8,128)(2,1)S(1)} %collective-permute-done.2.refs_1_, bf16[8,2,16,1024]{3,2,1,0:T(8,128)(2,1)S(1)} %hold.1.refs_2_, bf16[4,2,16,1024]{3,2,1,0:T(8,128)(2,1)} %collective-permute-done.5.refs_3_, ...), custom_call_target="tpu_custom_call" | custom-call | tf_op jit(solution)/shard_map/order_rows/pallas_call | solution.py:162
  84.5 0.0 copy-start.1
  84.5 0.0 copy-start.5
  84.6 0.3 fusion
  84.9 0.1 pad_maximum_fusion.right_ref
  85.0 0.0 collective-permute-done.7.last_ref
  85.0 0.8 copy-done.1
  85.8 0.0 copy-done.5
  85.8 3.8 %final_update.1 = (bf16[1024,512]{1,0:T(8,128)(2,1)}, bf16[64,1024]{1,0:T(8,128)(2,1)}, bf16[1024,1024]{1,0:T(8,128)(2,1)S(1)}) custom-call(s32[32,32]{1,0:T(8,128)S(1)} %copy-done.5, bf16[1024,1024]{1,0:T(8,128)(2,1)S(1)} %order_rows.1.rows_ref, bf16[8,2,16,1024]{3,2,1,0:T(8,128)(2,1)S(1)} %collective-permute-done.7.last_ref, ...), custom_call_target="tpu_custom_call", output_to_operand_aliasing={{2}: (1, {})} | custom-call | flops 1207959552 | bytes 6291456 | tf_op jit(solution)/shard_map/final_update/pallas_call | solution.py:201
  (6 shorter events, 0.1 us)
Async XLA Ops:
  0.6 1.3 %copy-start = (bf16[2,512,512]{2,1,0:T(8,128)(2,1)S(1)}, bf16[2,512,512]{2,1,0:T(8,128)(2,1)}, u32[]{:S(2)}) copy-start(bf16[2,512,512]{2,1,0:T(8,128)(2,1)} %param.9) | copy-start | bytes 3145732
  0.6 31.9 %copy-start.6 = (s32[32]{0:T(128)S(1)}, s32[32]{0:T(128)}, u32[]{:S(2)}) copy-start(s32[32]{0:T(128)} %colmap_ref.1) | copy-start | bytes 388
  0.7 47.9 %copy-start.2 = (bf16[64,512]{1,0:T(8,128)(2,1)S(1)}, bf16[64,512]{1,0:T(8,128)(2,1)}, u32[]{:S(2)}) copy-start(bf16[64,512]{1,0:T(8,128)(2,1)} %sketch_ref.1) | copy-start | bytes 196612
  0.7 47.9 %copy-start.4 = (bf16[2,64,512]{2,1,0:T(8,128)(2,1)S(1)}, bf16[2,64,512]{2,1,0:T(8,128)(2,1)}, u32[]{:S(2)}) copy-start(bf16[2,64,512]{2,1,0:T(8,128)(2,1)} %right_ref.1) | copy-start | bytes 393220
  0.7 47.9 %copy-start.3 = (bf16[1,64,1024]{2,1,0:T(8,128)(2,1)S(1)}, bf16[1,64,1024]{2,1,0:T(8,128)(2,1)}, u32[]{:S(2)}) copy-start(bf16[1,64,1024]{2,1,0:T(8,128)(2,1)} %param.11) | copy-start | bytes 393220
  2.3 30.2 %collective-permute-start = (bf16[1,2,16,1024]{3,2,1,0:T(8,128)(2,1)S(1)}, bf16[1,2,16,1024]{3,2,1,0:T(8,128)(2,1)S(1)}, u32[]{:S(2)}, u32[]{:S(2)}) collective-permute-start(bf16[1,2,16,1024]{3,2,1,0:T(8,128)(2,1)S(1)} %convert_element_type.25), channel_id=1, source_target_pairs={{0,256},{16,272},{32,288},{48,304},{64,320},{80,336},{96,352},{112... | collective-permute-start | bytes 196616 | tf_op jit(solution)/shard_map/ppermute | solution.py:30
  33.8 22.2 %all-to-all-start.1 = ((bf16[32,8,128]{2,1,0:T(8,128)(2,1)}), bf16[32,8,128]{2,1,0:T(8,128)(2,1)S(1)}, u32[]{:S(2)}, u32[]{:S(2)}) async-start(bf16[32,8,128]{2,1,0:T(8,128)(2,1)} %select_tiles.1._), calls=%async_computation.1 | async-start | bytes 131072 | tf_op jit(solution)/shard_map/all_to_all | solution.py:260
  41.3 14.7 %collective-permute-start.1 = (bf16[2,2,16,1024]{3,2,1,0:T(8,128)(2,1)S(1)}, bf16[2,2,16,1024]{3,2,1,0:T(8,128)(2,1)S(1)}, u32[]{:S(2)}, u32[]{:S(2)}) collective-permute-start(bf16[2,2,16,1024]{3,2,1,0:T(8,128)(2,1)S(1)} %constant_dynamic-update-slice_fusion.refs_0_), channel_id=1, source_target_pairs={{0,128},{16,400},{32,160},{48,432},{64,192},{80,464},{96,224},{112... | collective-permute-start | bytes 393224 | tf_op jit(solution)/shard_map/ppermute | solution.py:30
  57.2 23.3 %all-to-all-start.2 = ((bf16[16,32,8,128]{3,2,1,0:T(8,128)(2,1)}), bf16[16,32,8,128]{3,2,1,0:T(8,128)(2,1)S(1)}, u32[]{:S(2)}, u32[]{:S(2)}) async-start(bf16[16,32,8,128]{3,2,1,0:T(8,128)(2,1)} %spread.1), calls=%async_computation.2 | async-start | bytes 2097152 | tf_op jit(solution)/shard_map/all_to_all | solution.py:268
  60.8 14.1 %collective-permute-start.2 = (bf16[4,2,16,1024]{3,2,1,0:T(8,128)(2,1)S(1)}, bf16[4,2,16,1024]{3,2,1,0:T(8,128)(2,1)S(1)}, u32[]{:S(2)}, u32[]{:S(2)}) collective-permute-start(bf16[4,2,16,1024]{3,2,1,0:T(8,128)(2,1)S(1)} %stack_after.1.refs_0_), channel_id=1, source_target_pairs={{0,32},{16,48},{32,64},{48,80},{64,96},{80,112},{96,128},{112,144}... | collective-permute-start | bytes 786440 | tf_op jit(solution)/shard_map/ppermute | solution.py:30
  63.1 13.8 %collective-permute-start.4 = (bf16[4,2,16,1024]{3,2,1,0:T(8,128)(2,1)S(1)}, bf16[4,2,16,1024]{3,2,1,0:T(8,128)(2,1)S(1)}, u32[]{:S(2)}, u32[]{:S(2)}) collective-permute-start(bf16[4,2,16,1024]{3,2,1,0:T(8,128)(2,1)S(1)} %stack_after.1.refs_0_), channel_id=1, source_target_pairs={{0,64},{16,464},{32,96},{48,496},{64,128},{80,16},{96,160},{112,48... | collective-permute-start | bytes 786440 | tf_op jit(solution)/shard_map/ppermute | solution.py:30
  68.7 11.7 %collective-permute-start.3 = (bf16[4,2,16,1024]{3,2,1,0:T(8,128)(2,1)S(1)}, bf16[4,2,16,1024]{3,2,1,0:T(8,128)(2,1)S(1)}, u32[]{:S(2)}, u32[]{:S(2)}) collective-permute-start(bf16[4,2,16,1024]{3,2,1,0:T(8,128)(2,1)S(1)} %stack_after.1.refs_0_), channel_id=1, source_target_pairs={{0,480},{16,496},{32,0},{48,16},{64,32},{80,48},{96,64},{112,80},{... | collective-permute-start | bytes 786440 | tf_op jit(solution)/shard_map/ppermute | solution.py:30
  70.6 12.7 %collective-permute-start.5 = (bf16[4,2,16,1024]{3,2,1,0:T(8,128)(2,1)S(1)}, bf16[4,2,16,1024]{3,2,1,0:T(8,128)(2,1)}, u32[]{:S(2)}, u32[]{:S(2)}) collective-permute-start(bf16[4,2,16,1024]{3,2,1,0:T(8,128)(2,1)S(1)} %stack_after.1.refs_0_), channel_id=1, source_target_pairs={{0,16},{16,0},{32,48},{48,32},{64,80},{80,64},{96,112},{112,96},{1... | collective-permute-start | bytes 786440 | tf_op jit(solution)/shard_map/ppermute | solution.py:266
  75.0 8.4 %collective-permute-start.6 = (bf16[4,2,16,1024]{3,2,1,0:T(8,128)(2,1)S(1)}, bf16[4,2,16,1024]{3,2,1,0:T(8,128)(2,1)}, u32[]{:S(2)}, u32[]{:S(2)}) collective-permute-start(bf16[4,2,16,1024]{3,2,1,0:T(8,128)(2,1)S(1)} %collective-permute-done.2.refs_1_), channel_id=1, source_target_pairs={{0,16},{16,0},{32,48},{48,32},{64,80},{80,64},{96,112},{112,96},{1... | collective-permute-start | bytes 786440 | tf_op jit(solution)/shard_map/ppermute | solution.py:266
  80.6 4.4 %collective-permute-start.7 = (bf16[8,2,16,1024]{3,2,1,0:T(8,128)(2,1)S(1)}, bf16[8,2,16,1024]{3,2,1,0:T(8,128)(2,1)S(1)}, u32[]{:S(2)}, u32[]{:S(2)}) collective-permute-start(bf16[8,2,16,1024]{3,2,1,0:T(8,128)(2,1)S(1)} %hold.1.refs_2_), channel_id=1, source_target_pairs={{0,16},{16,0},{32,48},{48,32},{64,80},{80,64},{96,112},{112,96},{1... | collective-permute-start | bytes 1572872 | tf_op jit(solution)/shard_map/ppermute | solution.py:270
  84.5 1.2 %copy-start.1 = (bf16[1024,512]{1,0:T(8,128)(2,1)S(1)}, bf16[1024,512]{1,0:T(8,128)(2,1)}, u32[]{:S(2)}) copy-start(bf16[1024,512]{1,0:T(8,128)(2,1)} %tiles_ref.1) | copy-start | bytes 3145732
  84.5 1.2 %copy-start.5 = (s32[32,32]{1,0:T(8,128)S(1)}, s32[32,32]{1,0:T(8,128)}, u32[]{:S(2)}) copy-start(s32[32,32]{1,0:T(8,128)} %pattern_ref.1) | copy-start | bytes 12292
